TPU v7x, 128 devices: a whole 4x4x4 slice. The times are simulated.
128 devices in a mesh: side: 2 (over core), dev: 64 (over y, x, z).
Axes of the slice: x: 4, y: 4, z: 4, core: 2. Of those that a mesh axis runs over, the one named last changes fastest.
Arguments:
- queries: bfloat16 [1024, 128, 576], P(('side', 'dev'))
- cache: bfloat16 [1024, 512, 576], P(('side', 'dev'))
- lengths: int32 [1024], P(('side', 'dev')), may hold values from 2 to 512, as said below
- w_uv: bfloat16 [128, 512, 128], P(('side', 'dev')), may hold values from -0.25 to 0.25
- w_out: bfloat16 [16384, 7168], P(('side', 'dev')), may hold values from -0.046875 to 0.046875
- resid: bfloat16 [1024, 7168], P(('side', 'dev')), may hold values from -6 to 6
- norm_gain: float32 [7168], replicated, may hold values from 0.1 to 1.9
- expert_ids: int32 [1024, 4], P(('side', 'dev')), may hold values from 0 to 23, all different within a row; in each aligned block of 8 rows (0 to 7, 8 to 15, ...) at most 2 rows name the same one
- gate_weights: bfloat16 [1024, 4], P(('side', 'dev')), may hold values from 0.099609375 to 1
- replica_slot: int32 [24, 2], replicated, may hold values from 0 to 31, as said below
- w_gate: bfloat16 [128, 7168, 256], P(('side', 'dev')), as said below
- w_up: bfloat16 [128, 7168, 256], P(('side', 'dev')), as said below
- w_down: bfloat16 [128, 256, 7168], P(('side', 'dev')), as said below
Outputs:
- attended: bfloat16 [1024, 7168], P(('side', 'dev'))
- layer_out: bfloat16 [1024, 7168], P(('side', 'dev'))
Inputs may be any that keep to these rules, and one draw needn't show every extreme that they name: `lengths`: each request has at least two valid slots; some request uses all 512. `expert_ids`: among the 8 requests of one device (aligned blocks) no expert is chosen more than 2 times, and some expert is chosen exactly 2 times. `replica_slot`: column 0 of expert e is slot e. 8 experts have a second replica in the slots 24 to 31, one each; for the others column 1 equals column 0. `w_gate`: entries of two slots that hold the same expert are equal, quarter by quarter. `w_up`: as for w_gate. `w_down`: as for w_gate.
All inputs are finite; a program needn't handle non-finite values.
Results may differ from a plain program's by a relative error of at most 0.015.
Values may be sent and summed in bfloat16 or wider, within the bound.
A program may use at most 192 MiB of HBM per device.

v0:
```python
import math

import jax
import jax.numpy as jnp
from jax import lax
from jax.sharding import PartitionSpec as P

GROUP = 4


def local(
    queries,
    cache,
    lengths,
    w_uv,
    w_out,
    resid,
    norm_gain,
    expert_ids,
    gate_weights,
    replica_slot,
    w_gate,
    w_up,
    w_down,
):
    n_all = lax.axis_size(("side", "dev"))
    my_index = lax.axis_index(("side", "dev"))
    r_dev, top_count = expert_ids.shape
    width = resid.shape[1]
    latent_width = w_uv.shape[1]
    value_width = w_uv.shape[2]
    key_width = queries.shape[2]
    slot_count = n_all // GROUP
    expert_count = replica_slot.shape[0]
    capacity = min(r_dev, max(2, 2 * r_dev * top_count // expert_count))
    score_scale = 1.0 / math.sqrt(value_width + key_width - latent_width)
    scores = (
        jnp.einsum("rhk,rjk->rhj", queries, cache, preferred_element_type=jnp.float32) * score_scale
    )
    valid_key = jnp.arange(cache.shape[1], dtype=jnp.int32)[None, None, :] < lengths[:, None, None]
    scores = jnp.where(valid_key, scores, -1e30)
    highest = jnp.max(scores, axis=2, keepdims=True)
    exponent = jnp.exp(scores - highest)
    weights = (exponent / jnp.sum(exponent, axis=2, keepdims=True)).astype(jnp.bfloat16)
    latent = jnp.einsum(
        "rhj,rjc->rhc", weights, cache[:, :, :latent_width], preferred_element_type=jnp.float32
    ).astype(jnp.bfloat16)
    head_rows = lax.all_to_all(latent, ("side", "dev"), split_axis=1, concat_axis=0, tiled=True)
    local_heads = head_rows.shape[1]
    values = jnp.einsum("rhc,hce->rhe", head_rows, w_uv, preferred_element_type=jnp.float32).astype(
        jnp.bfloat16
    )
    values = values.reshape(head_rows.shape[0], local_heads * value_width)
    attention = lax.psum_scatter(
        jnp.dot(values, w_out, preferred_element_type=jnp.float32),
        ("side", "dev"),
        scatter_dimension=0,
        tiled=True,
    )
    attended = (resid.astype(jnp.float32) + attention).astype(jnp.bfloat16)
    stream = attended.astype(jnp.float32)
    normed = (
        stream * lax.rsqrt(jnp.mean(stream * stream, axis=1, keepdims=True) + 1e-06) * norm_gain
    ).astype(jnp.bfloat16)
    req_index = my_index * r_dev + jnp.arange(r_dev, dtype=jnp.int32)
    parity = (req_index[:, None] + jnp.arange(top_count, dtype=jnp.int32)[None, :]) % 2
    matches = expert_ids[:, :, None] == jnp.arange(expert_count, dtype=jnp.int32)[None, None, :]
    first_slot = jnp.sum(jnp.where(matches, replica_slot[:, 0][None, None, :], 0), axis=2)
    second_slot = jnp.sum(jnp.where(matches, replica_slot[:, 1][None, None, :], 0), axis=2)
    pair_slot = jnp.where(parity == 1, second_slot, first_slot).reshape(-1)
    onehot = pair_slot[:, None] == jnp.arange(slot_count, dtype=jnp.int32)[None, :]
    slot_rank = jnp.cumsum(onehot.astype(jnp.int32), axis=0) - 1
    pair_rank = jnp.sum(jnp.where(onehot, slot_rank, 0), axis=1)
    target = pair_slot * capacity + pair_rank
    select = target[None, :] == jnp.arange(slot_count * capacity, dtype=jnp.int32)[:, None]
    pair_rows = jnp.repeat(normed, top_count, axis=0)
    slot_rows = jnp.dot(
        select.astype(jnp.bfloat16), pair_rows, preferred_element_type=jnp.float32
    ).astype(jnp.bfloat16)
    pair_gate = gate_weights.reshape(-1)
    slot_gates = jnp.sum(jnp.where(select, pair_gate[None, :], jnp.zeros((), jnp.bfloat16)), axis=1)
    send_rows = jnp.broadcast_to(
        slot_rows.reshape(slot_count, 1, capacity, width), (slot_count, GROUP, capacity, width)
    ).reshape(n_all, capacity, width)
    send_gates = jnp.broadcast_to(
        slot_gates.reshape(slot_count, 1, capacity), (slot_count, GROUP, capacity)
    ).reshape(n_all, capacity)
    rows_in = lax.all_to_all(send_rows, ("side", "dev"), split_axis=0, concat_axis=0, tiled=True)
    flat_rows = rows_in.reshape(-1, width)
    gate_proj = jnp.dot(flat_rows, w_gate[0], preferred_element_type=jnp.float32)
    up_proj = jnp.dot(flat_rows, w_up[0], preferred_element_type=jnp.float32)
    hidden = (jax.nn.silu(gate_proj) * up_proj).astype(jnp.bfloat16)
    output = jnp.dot(hidden, w_down[0], preferred_element_type=jnp.float32) * lax.all_to_all(
        send_gates, ("side", "dev"), split_axis=0, concat_axis=0, tiled=True
    ).reshape(-1)[:, None].astype(jnp.float32)
    pieces = output.astype(jnp.bfloat16).reshape(rows_in.shape)
    returned = lax.all_to_all(pieces, ("side", "dev"), split_axis=0, concat_axis=0, tiled=True)
    summed = jnp.sum(
        returned.reshape(slot_count, GROUP, capacity, width).astype(jnp.float32), axis=1
    ).reshape(slot_count * capacity, width)
    token_select = jnp.sum(
        select.reshape(slot_count * capacity, r_dev, top_count).astype(jnp.float32), axis=2
    )
    moe = jnp.dot(token_select.T, summed, precision=lax.Precision.HIGHEST)
    layer_out = (stream + moe).astype(jnp.bfloat16)
    return (attended, layer_out)


def solution(mesh):
    return jax.shard_map(
        local,
        mesh=mesh,
        in_specs=(
            P(("side", "dev"), None, None),
            P(("side", "dev"), None, None),
            P(("side", "dev")),
            P(("side", "dev"), None, None),
            P(("side", "dev"), None),
            P(("side", "dev"), None),
            P(),
            P(("side", "dev"), None),
            P(("side", "dev"), None),
            P(),
            P(("side", "dev"), None, None),
            P(("side", "dev"), None, None),
            P(("side", "dev"), None, None),
        ),
        out_specs=(P(("side", "dev"), None), P(("side", "dev"), None)),
        check_vma=False,
    )
```

profile of v0, /device:TPU:1, one launch (start us, length us, event | category | flops | bytes accessed | tf_op | source)
XLA Modules:
  0.0 938.9 jit_solution(14014324604169262040)
XLA Ops:
  7.2 0.9 iota_compare_fusion.5
  8.1 3.8 fusion.56
  11.8 1.3 copy-done.2
  13.2 0.7 fusion.55
  13.9 4.9 fusion.11
  18.8 0.6 copy.33
  19.4 29.0 %all_to_all.34 = bf16[8,128,512]{2,0,1:T(8,128)(2,1)S(1)} all-to-all(bf16[8,128,512]{2,0,1:T(8,128)(2,1)S(1)} %copy.33), channel_id=1, replica_groups=mesh['side'=2,'dev'=64] {'side','dev'}, dimensions={1} | all-to-all | bytes 2097152 | tf_op jit(solution)/shard_map/all_to_all | solution.py:48
  48.4 12.0 %fusion.20 = f32[1024,7168]{1,0:T(8,128)} fusion(bf16[128,7168]{1,0:T(8,128)(2,1)S(1)} %copy-done, bf16[8,128,512]{2,0,1:T(8,128)(2,1)S(1)} %all_to_all.34, bf16[1,512,128]{2,1,0:T(8,128)(2,1)S(1)} %copy-done.4), kind=kOutput, calls=%fused_computation.22 | convolution fusion | flops 2013396992 | bytes 32374784 | tf_op jit(solution)/shard_map/dot_general | solution.py:55
  60.5 0.6 copy-done.9
  61.1 0.3 select_reduce_fusion.1
  61.4 0.1 copy.35
  61.5 0.1 reduce_sum.84
  61.6 0.1 copy.36
  61.6 0.1 reduce_sum.85
  61.8 0.1 copy.34
  61.8 0.1 add.96
  61.9 0.1 copy.38
  62.0 0.1 broadcast_in_dim.93
  62.2 0.2 select_reduce_fusion
  62.4 0.1 fusion.42
  62.5 0.1 broadcast_in_dim.96
  62.7 0.1 copy.39
  62.8 0.1 all_to_all.27
  63.0 0.8 copy.40
  63.7 5.7 all-to-all-start.2
  69.5 701.3 %reduce-scatter.2.cloned.1.call-done = f32[8,7168]{1,0:T(8,128)} async-done(((f32[1024,7168]{1,0:T(8,128)}), f32[8,7168]{1,0:T(8,128)}) %reduce-scatter.2.cloned.1.call-update) | async-done | bytes 229392 | tf_op jit(solution)/shard_map/reduce_scatter | solution.py:54
  770.7 1.1 fusion.34
  771.9 0.1 fusion.36
  772.0 0.1 broadcast_in_dim.90
  772.1 0.1 reshape.176
  772.2 0.5 convolution_convert_fusion
  772.7 0.3 broadcast_in_dim.91
  773.1 3.7 broadcast_in_dim.92
  776.8 5.1 all-to-all-start.1
  781.9 0.2 convert_reduce_fusion.1
  782.1 0.1 reshape.181
  782.3 44.7 %all-to-all-done.1 = bf16[128,2,7168]{2,1,0:T(2,128)(2,1)} async-done(((bf16[128,2,7168]{2,1,0:T(2,128)(2,1)}), bf16[128,2,7168]{2,1,0:T(2,128)(2,1)}, u32[]{:S(2)}, u32[]{:S(2)}) %all-to-all-start.1) | async-done | bytes 3670048 | tf_op jit(solution)/shard_map/all_to_all | solution.py:88
  826.9 8.4 reshape.178
  835.3 4.3 fusion.8
  839.6 10.0 %fusion.1 = bf16[256,7168]{1,0:T(8,128)(2,1)} fusion(bf16[1,256,7168]{2,1,0:T(8,128)(2,1)} %param.25, f32[256]{0:T(256)S(1)} %reshape.181, bf16[256,7168]{1,0:T(8,128)(2,1)} %reshape.178, bf16[1,7168,256]{2,1,0:T(8,128)(2,1)} %param.24, f32[256,256]{1,0:T(8,128)S(1)} %fusion.8), kind=kOutput, calls=%fused_computation.2 | convolution fusion | flops 1883111424 | bytes 14943232 | tf_op jit(solution)/shard_map/dot_general | solution.py:93
  849.6 8.1 reshape.179
  857.8 14.7 %all-to-all-start.3 = ((bf16[128,2,7168]{2,1,0:T(2,128)(2,1)}), bf16[128,2,7168]{2,1,0:T(2,128)(2,1)}, u32[]{:S(2)}, u32[]{:S(2)}) async-start(bf16[128,2,7168]{2,1,0:T(2,128)(2,1)} %reshape.179), calls=%async_computation.4 | async-start | bytes 7340032 | tf_op jit(solution)/shard_map/all_to_all | solution.py:97
  872.5 0.1 reduce_sum.87
  872.5 0.1 copy.37
  872.7 44.7 %all-to-all-done.3 = bf16[128,2,7168]{2,1,0:T(2,128)(2,1)} async-done(((bf16[128,2,7168]{2,1,0:T(2,128)(2,1)}), bf16[128,2,7168]{2,1,0:T(2,128)(2,1)}, u32[]{:S(2)}, u32[]{:S(2)}) %all-to-all-start.3) | async-done | bytes 3670048 | tf_op jit(solution)/shard_map/all_to_all | solution.py:97
  917.5 8.0 convert_reduce_fusion
  925.4 3.5 reshape.180
  928.9 3.1 fusion.2
  (32 shorter events, 0.4 us)
Async XLA Ops:
  7.2 41.2 %copy-start = (bf16[128,7168]{1,0:T(8,128)(2,1)S(1)}, bf16[128,7168]{1,0:T(8,128)(2,1)}, u32[]{:S(2)}) copy-start(bf16[128,7168]{1,0:T(8,128)(2,1)} %param.17) | copy-start | bytes 5505028
  7.2 763.5 %reduce-scatter.2.cloned.1.call-start = ((), (), s32[]{:S(2)}) async-start(), calls=%async_computation.5 | async-start | bytes 29589504 | tf_op jit(solution)/shard_map/reduce_scatter | solution.py:54
  11.8 1.4 copy-start.2
  18.8 29.6 %copy-start.4 = (bf16[1,512,128]{2,1,0:T(8,128)(2,1)S(1)}, bf16[1,512,128]{2,1,0:T(8,128)(2,1)}, u32[]{:S(2)}) copy-start(bf16[1,512,128]{2,1,0:T(8,128)(2,1)} %param.16) | copy-start | bytes 393220
  60.4 0.7 copy-start.9
  60.4 0.7 copy-start.7
  60.4 1.5 copy-start.8
  60.4 710.3 %copy-start.5 = (bf16[8,7168]{1,0:T(8,128)(2,1)S(1)}, bf16[8,7168]{1,0:T(8,128)(2,1)}, u32[]{:S(2)}) copy-start(bf16[8,7168]{1,0:T(8,128)(2,1)} %param.18) | copy-start | bytes 344068
  60.4 711.4 %copy-start.6 = (f32[7168]{0:T(1024)S(1)}, f32[7168]{0:T(1024)}, u32[]{:S(2)}) copy-start(f32[7168]{0:T(1024)} %param.19) | copy-start | bytes 86020
  63.7 709.3 %all-to-all-start.2 = ((bf16[128,1,2]{2,1,0:T(2,128)(2,1)}), bf16[128,1,2]{2,1,0:T(2,128)(2,1)S(1)}, u32[]{:S(2)}, u32[]{:S(2)}) async-start(bf16[128,1,2]{2,1,0:T(2,128)(2,1)} %copy.40), calls=%async_computation.3 | async-start | bytes 131072 | tf_op jit(solution)/shard_map/all_to_all | solution.py:93
  771.8 157.1 %copy-start.3 = (bf16[8,7168]{1,0:T(8,128)(2,1)}, bf16[8,7168]{1,0:T(8,128)(2,1)S(1)}, u32[]{:S(2)}) copy-start(bf16[8,7168]{1,0:T(8,128)(2,1)S(1)} %get-tuple-element.5) | copy-start | bytes 344068
  776.8 50.2 %all-to-all-start.1 = ((bf16[128,2,7168]{2,1,0:T(2,128)(2,1)}), bf16[128,2,7168]{2,1,0:T(2,128)(2,1)}, u32[]{:S(2)}, u32[]{:S(2)}) async-start(bf16[128,2,7168]{2,1,0:T(2,128)(2,1)} %bitcast.45), calls=%async_computation.2 | async-start | bytes 7340032 | tf_op jit(solution)/shard_map/all_to_all | solution.py:88
  857.8 59.7 %all-to-all-start.3 = ((bf16[128,2,7168]{2,1,0:T(2,128)(2,1)}), bf16[128,2,7168]{2,1,0:T(2,128)(2,1)}, u32[]{:S(2)}, u32[]{:S(2)}) async-start(bf16[128,2,7168]{2,1,0:T(2,128)(2,1)} %reshape.179), calls=%async_computation.4 | async-start | bytes 7340032 | tf_op jit(solution)/shard_map/all_to_all | solution.py:97
  917.5 14.5 %copy-start.1 = (bf16[128,7168]{1,0:T(8,128)(2,1)S(1)}, bf16[128,7168]{1,0:T(8,128)(2,1)}, u32[]{:S(2)}) copy-start(bf16[128,7168]{1,0:T(8,128)(2,1)} %param.17) | copy-start | bytes 5505028
Sparse Core Ops, SparseCore 0:
  60.6 710.0 reduce-scatter.1
where the time goes:
time: 946 us; the launch traced here: 939 us
  waiting for transfers between devices  791 us (84%)
  matrix products  38.6 us (4%)
  local copies, waits for them, and re-layouts  29.1 us (3%)
  blocking collectives  29 us (3%)
  starting transfers between devices  25.6 us (3%)
  between operations  14.3 us (2%)
  other arithmetic  11.7 us (1%)
    reduce_scatter x1, waiting for transfers between devices, local(): lax.psum_scatter(jnp.dot(values, w_out, preferred_element_type=jnp.float3...  701 us
    all_to_all x1, waiting for transfers between devices, local(): lax.all_to_all(pieces, ('side', 'dev'), split_axis=0, concat_axis=0, tile...  44.7 us
    all_to_all x1, waiting for transfers between devices, local(): lax.all_to_all(send_rows, ('side', 'dev'), split_axis=0, concat_axis=0, t...  44.7 us
    all_to_all x1, blocking collectives, local(): lax.all_to_all(latent, ('side', 'dev'), split_axis=1, concat_axis=0, tile...  29 us
  transfers between devices with their start and end apart: 4, of which 3 were waited for; matrix products, arithmetic and copies ran while one was open for 1% of the time, Pallas kernels for 0%

commit v1 on v0

v1 whole, which is shorter than its diff:
```python
import functools
import math

import jax
import jax.numpy as jnp
from jax import lax
from jax.experimental import pallas as pl
from jax.experimental.pallas import tpu as pltpu
from jax.sharding import PartitionSpec as P

GROUP = 4
BF = jnp.bfloat16
F32 = jnp.float32
MB = 1 << 20


def place():
    s = lax.axis_index("side")
    dev = lax.axis_index("dev")
    return s, dev // 4, dev % 4


def dot(a, b, dims=((1,), (0,))):
    return lax.dot_general(a, b, (dims, ((), ())), preferred_element_type=F32)


def send(src, dst, ssem, rsem, s, yx, z):
    pltpu.make_async_remote_copy(
        src_ref=src,
        dst_ref=dst,
        send_sem=ssem,
        recv_sem=rsem,
        device_id=(s, yx * 4 + z),
        device_id_type=pl.DeviceIdType.MESH,
    ).start()


def keep(src, dst, sem):
    pltpu.make_async_copy(src, dst, sem).start()


def wait(ref, sem):
    pltpu.make_async_copy(ref, ref, sem).wait()


def around(yx, k):
    return ((yx // 4 + k // 4) % 4) * 4 + (yx % 4 + k % 4) % 4


def iota(shape, dim):
    return lax.broadcasted_iota(jnp.int32, shape, dim)


def attention_phase(
    lengths, queries, cache, w_uv, w_out, resid,
    cbuf, late, lrecv, wuv, wo, vals, osend, orecv, rsend, rrecv, gathered,
    csem, ssem, rsem, vsem, osem,
):
    s, yx, z = place()
    for r in range(8):
        pltpu.make_async_copy(cache.at[r], cbuf.at[r], csem.at[r]).start()
    own_col = pl.multiple_of((s * 4 + z) * 128, 128)
    keep(w_uv, wuv.at[:, pl.ds(own_col, 128)], rsem.at[0])
    keep(w_out.at[:, pl.ds(pl.multiple_of(z * 1792, 256), 1792)], wo.at[pl.ds(own_col, 128)], rsem.at[1])
    for q in range(4):
        rsend[q] = resid[:, q * 1792 : (q + 1) * 1792].astype(F32)
    for k in (1, 3, 2):
        send(w_uv, wuv.at[:, pl.ds(own_col, 128)], ssem.at[0], rsem.at[0], s, yx, (z + k) % 4)
    for k in (1, 3, 2):
        t = (z + k) % 4
        send(
            w_out.at[:, pl.ds(pl.multiple_of(t * 1792, 256), 1792)],
            wo.at[pl.ds(own_col, 128)],
            ssem.at[1], rsem.at[1], s, yx, t,
        )
    keep(rsend.at[z], rrecv.at[z], rsem.at[2])
    for k in (1, 3, 2):
        t = (z + k) % 4
        send(rsend.at[t], rrecv.at[z], ssem.at[2], rsem.at[2], s, yx, t)

    row, col = iota((128, 128), 0), iota((128, 128), 1)
    head = ((row % 8) // 4) * 64 + (row // 8) * 4 + row % 4
    order = jnp.where(col == head, 1.0, 0.0).astype(BF)
    scale = 1.0 / math.sqrt(192)
    column = iota((128, 512), 1)

    def one(r):
        wait(cbuf.at[r], csem.at[r])
        q = dot(order, queries[r], ((1,), (1,))).astype(BF)
        scores = dot(q, cbuf[r]) * scale
        scores = jnp.where(column < lengths[r], scores, -1e30)
        weight = jnp.exp(scores - jnp.max(scores, axis=1, keepdims=True))
        total = jnp.sum(weight, axis=1, keepdims=True)
        latent = dot(weight.astype(BF), cbuf[r, 0:512], ((1,), (1,)))
        return (latent / total).reshape(16, 8, 512)

    def step(i, carry):
        late[i] = jnp.concatenate([one(2 * i), one(2 * i + 1)], axis=1).astype(BF)
        keep(late.at[i, yx], lrecv.at[yx, i], rsem.at[5])

        def out(k, carry):
            to = around(yx, k)
            send(late.at[i, to], lrecv.at[yx, i], ssem.at[5], rsem.at[5], s, to, z)
            return carry

        return lax.fori_loop(1, 16, out, carry)

    lax.fori_loop(0, 4, step, 0)

    half = pl.ds(pl.multiple_of(s * 512, 512), 512)
    wait(wuv.at[:, half], rsem.at[0])
    send(wuv.at[:, half], wuv.at[:, half], ssem.at[3], rsem.at[3], 1 - s, yx, z)
    wait(wuv.at[:, half], rsem.at[3])
    wait(lrecv, rsem.at[5])

    mine = iota((256, 1024), 0) % 8 == iota((256, 1024), 1) // 128
    pick = jnp.where(iota((32, 256), 1) // 8 == iota((32, 256), 0), 1.0, 0.0).astype(BF)

    def value(j, carry):
        rows = lrecv[pl.ds(j * 4, 4)].reshape(256, 512)
        full = dot(rows, wuv[...])
        own = jnp.where(mine, full, 0.0).astype(BF)
        vals[z, j] = dot(pick, own).astype(BF)
        for k in (1, 3, 2):
            send(vals.at[z, j], vals.at[z, j], ssem.at[6], vsem.at[z], s, yx, (z + k) % 4)
        return carry

    lax.fori_loop(0, 4, value, 0)

    wait(wo.at[half], rsem.at[1])
    send(wo.at[half], wo.at[half], ssem.at[4], rsem.at[4], 1 - s, yx, z)
    wait(wo.at[half], rsem.at[4])

    for pp in range(2):
        p = (z // 2 + pp) % 2
        for e in range(2):
            @pl.when(2 * p + e != z)
            def _():
                wait(vals.at[2 * p + e], vsem.at[2 * p + e])

        def project(c, carry):
            at = pl.ds(pl.multiple_of(c * 256, 256), 256)
            got = dot(vals[pl.ds(2 * p, 2)].reshape(256, 1024), wo[:, at]).reshape(2, 16, 8, 256)
            osend[p, :, :, at] = jnp.concatenate([got[0], got[1]], axis=1).astype(BF)
            return carry

        lax.fori_loop(0, 7, project, 0)
        keep(osend.at[p, yx], orecv.at[p, yx], osem.at[p])

        def out(k, carry):
            to = around(yx, k)
            send(osend.at[p, to], orecv.at[p, yx], ssem.at[7], osem.at[p], s, to, z)
            return carry

        lax.fori_loop(1, 16, out, 0)

    here = pl.ds(pl.multiple_of(z * 1792, 256), 1792)
    for pp in range(2):
        p = (z // 2 + pp) % 2
        wait(orecv.at[p], osem.at[p])
        if pp == 0:
            wait(rrecv, rsem.at[2])
        total = jnp.concatenate([rrecv[2 * p], rrecv[2 * p + 1]], axis=0)
        summed = lax.fori_loop(0, 16, lambda i, a: a + orecv[p, i].astype(F32), jnp.zeros((16, 1792), F32))
        gathered[s, pl.ds(pl.multiple_of(p * 16, 16), 16), here] = (total + summed).astype(BF)

    for k in (1, 3, 2):
        send(gathered.at[s, :, here], gathered.at[s, :, here], ssem.at[8], rsem.at[8], s, yx, (z + k) % 4)
    wait(gathered.at[s, :, pl.ds(0, 5376)], rsem.at[8])
    send(gathered.at[s], gathered.at[s], ssem.at[9], rsem.at[9], 1 - s, yx, z)
    wait(gathered.at[s], rsem.at[9])

    for ref, number in (
        (wuv.at[:, pl.ds(0, 384)], 0),
        (wo.at[pl.ds(0, 384)], 1),
        (rsend.at[pl.ds(0, 3)], 2),
        (wuv.at[:, half], 3),
        (wo.at[half], 4),
        (late.at[:, pl.ds(0, 15)], 5),
        (vals.at[pl.ds(0, 3)], 6),
        (osend.at[:, pl.ds(0, 15)], 7),
        (gathered.at[s, :, pl.ds(0, 5376)], 8),
        (gathered.at[s], 9),
    ):
        wait(ref, ssem.at[number])


def attention_kernel(lengths, queries, cache, w_uv, w_out, resid, gathered, *scratch):
    attention_phase(lengths, queries, cache, w_uv, w_out, resid, *scratch[:10], gathered, *scratch[10:])


VMEM = pl.BlockSpec(memory_space=pltpu.VMEM)
SMEM = pl.BlockSpec(memory_space=pltpu.SMEM)
ANY = pl.BlockSpec(memory_space=pl.ANY)


def attention_scratch():
    return [
        pltpu.VMEM((8, 576, 512), BF),
        pltpu.VMEM((4, 16, 16, 512), BF),
        pltpu.VMEM((16, 4, 16, 512), BF),
        pltpu.VMEM((512, 1024), BF),
        pltpu.VMEM((1024, 1792), BF),
        pltpu.VMEM((4, 4, 32, 1024), BF),
        pltpu.VMEM((2, 16, 16, 1792), BF),
        pltpu.VMEM((2, 16, 16, 1792), BF),
        pltpu.VMEM((4, 8, 1792), F32),
        pltpu.VMEM((4, 8, 1792), F32),
    ]


def attention_call(lengths, queries, cache, w_uv, w_out, resid):
    return pl.pallas_call(
        attention_kernel,
        out_shape=jax.ShapeDtypeStruct((2, 32, 7168), BF),
        in_specs=[SMEM, VMEM, ANY, ANY, ANY, VMEM],
        out_specs=VMEM,
        scratch_shapes=attention_scratch()
        + [pltpu.SemaphoreType.DMA((n,)) for n in (8, 10, 10, 4, 2)],
        compiler_params=pltpu.CompilerParams(has_side_effects=True, vmem_limit_bytes=56 * MB),
        name="attention",
    )(lengths, jnp.swapaxes(queries, 1, 2), jnp.swapaxes(cache, 1, 2), w_uv[0], w_out, resid)


def expert_phase(
    expert_ids, gates, replicas, gain, w_gate, w_up, w_down, gathered, attended, layer_out,
    wg, wu, wd, route, normed, select, picked, rows, acc, hidden, ysend, yrecv, bsend, asend, back, part, fsend, frecv,
    wsem, ssem, rsem, xsem, ysem, bsem,
):
    s, yx, z = place()
    keep(w_gate, wg, wsem.at[0])
    keep(w_up, wu, wsem.at[1])
    keep(w_down, wd, wsem.at[2])
    slot_me = s * 16 + yx
    line_me = s * 4 + z

    row, lane = iota((64, 128), 0), iota((64, 128), 1)

    def choice(p, carry):
        table, used = carry
        t, k = p // 4, p % 4
        slot = replicas[expert_ids[t, k], (t + k) % 2]
        same = row // 2 == slot
        hit = same & (row % 2 == used)
        table = jnp.where(hit & (lane == line_me * 8 + t), 1.0, table)
        table = jnp.where(hit & (lane == 64 + line_me * 8 + t), gates[t, k], table)
        return table, used + jnp.where(same, 1, 0)

    table, _ = lax.fori_loop(0, 32, choice, (jnp.zeros((64, 128), F32), jnp.zeros((64, 128), jnp.int32)))
    route[line_me] = table.astype(BF)

    def announce(k, carry):
        send(route.at[line_me], route.at[line_me], ssem.at[0], rsem.at[0], (s + k // 4) % 2, yx, (z + k % 4) % 4)
        return carry

    lax.fori_loop(1, 8, announce, 0)

    def norm(b, carry):
        at = pl.ds(pl.multiple_of((b % 2) * 16, 16), 16)
        stream = gathered[b // 2, at].astype(F32)
        mean = jnp.mean(stream * stream, axis=1, keepdims=True)
        normed[pl.ds(pl.multiple_of(b * 16, 16), 16)] = (stream * lax.rsqrt(mean + 1e-06) * gain[...]).astype(BF)
        return carry

    lax.fori_loop(0, 4, norm, 0)

    wait(route.at[pl.ds(0, 7)], rsem.at[0])
    a, b = iota((512, 512), 0), iota((512, 512), 1)
    deal = jnp.where(b == ((a % 16) // 2) * 64 + (a // 16) * 2 + a % 2, 1.0, 0.0).astype(BF)
    select[...] = dot(deal, route[...].reshape(512, 128)).astype(BF)

    for c in range(4):
        first = (z * 2 + s) * 512 if c == 0 else 4096 + s * 1536 + (c - 1) * 512
        cols = pl.ds(pl.multiple_of(first, 512), 512)
        picked[c] = dot(select[:, 0:64], normed[:, cols]).astype(BF).reshape(32, 16, 512)
        number = 1 if c == 0 else 2
        place_in = rows.at[pl.ds(pl.multiple_of(yx * 16, 16), 16), cols]
        keep(picked.at[c, slot_me], place_in, rsem.at[number])

        def out(k, carry):
            to, core = around(yx, k // 2), (s + k % 2) % 2
            send(picked.at[c, core * 16 + to], place_in, ssem.at[number], rsem.at[number], core, to, z)
            return carry

        lax.fori_loop(1, 32, out, 0)

    own = pl.ds(pl.multiple_of(z * 1024, 1024), 1024)
    wait(rows.at[:, own], rsem.at[1])
    for k in (1, 3, 2):
        send(rows.at[:, own], rows.at[:, own], ssem.at[3], xsem.at[z], s, yx, (z + k) % 4)

    wait(wg, wsem.at[0])
    wait(wu, wsem.at[1])
    acc[...] = jnp.zeros_like(acc)

    def project(c, carry):
        at = pl.ds(pl.multiple_of(c * 1024, 1024), 1024)
        acc[0] += dot(rows[:, at], wg[at])
        acc[1] += dot(rows[:, at], wu[at])
        return carry

    project(z, 0)
    for k in (1, 3, 2):
        t = (z + k) % 4
        wait(rows.at[:, pl.ds(pl.multiple_of(t * 1024, 1024), 1024)], xsem.at[t])
        project(t, 0)
    wait(rows.at[:, pl.ds(4096, 3072)], rsem.at[2])
    lax.fori_loop(4, 7, project, 0)
    gate = acc[0]
    hidden[...] = (gate * jax.nn.sigmoid(gate) * acc[1]).astype(BF)
    wait(wd, wsem.at[2])

    for k in (1, 3, 2, 0):
        t = (z + k) % 4
        at = pl.ds(pl.multiple_of(t * 1024, 1024), 1024)
        got = dot(hidden[...], wd[:, at]).astype(BF)
        if k == 0:
            yrecv[z] = got
        else:
            ysend[t] = got
            send(ysend.at[t], yrecv.at[z], ssem.at[4], ysem.at[z], s, yx, t)

    def give_back(source, core, c):
        keep_here = core == s

        @pl.when(keep_here)
        def _():
            keep(source.at[pl.ds(pl.multiple_of(yx * 16, 16), 16)], back.at[c, slot_me], bsem.at[c])

        @pl.when(jnp.logical_not(keep_here))
        def _():
            send(source.at[pl.ds(pl.multiple_of(yx * 16, 16), 16)], back.at[c, slot_me], ssem.at[5], bsem.at[c], core, yx, z)

        def out(k, carry):
            to = around(yx, k)
            send(source.at[pl.ds(pl.multiple_of(to * 16, 16), 16)], back.at[c, slot_me], ssem.at[5], bsem.at[c], core, to, z)
            return carry

        lax.fori_loop(1, 16, out, 0)

    for c in range(3):
        for core in range(2):
            j = core * 3 + c
            bsend[j] = dot(hidden[...], wd[:, 4096 + j * 512 : 4608 + j * 512]).astype(BF)
            give_back(bsend.at[j], core, c)

    for k in (1, 3, 2):
        wait(yrecv.at[(z + k) % 4], ysem.at[(z + k) % 4])
    for core in range(2):
        at = pl.ds(core * 512, 512)
        total = (yrecv[0, :, at].astype(F32) + yrecv[1, :, at].astype(F32)) + (
            yrecv[2, :, at].astype(F32) + yrecv[3, :, at].astype(F32)
        )
        asend[core] = total.astype(BF)
        give_back(asend.at[core], core, 3)

    for c in range(4):
        wait(back.at[c], bsem.at[c])
        part[c] = dot(select[...], back[c].reshape(512, 512), ((0,), (0,)))[64:128]

    def pair(c, d):
        return jnp.concatenate([part[c].reshape(8, 8, 512), part[d].reshape(8, 8, 512)], axis=1).astype(BF)

    fsend[:, :, 0:512] = pair(3, 1)
    fsend[:, :, 512:1024] = pair(0, 2)
    keep(fsend.at[line_me], frecv.at[line_me], rsem.at[6])

    def finish(k, carry):
        core, to = (s + k // 4) % 2, (z + k % 4) % 4
        send(fsend.at[core * 4 + to], frecv.at[line_me], ssem.at[6], rsem.at[6], core, yx, to)
        return carry

    lax.fori_loop(1, 8, finish, 0)
    wait(frecv, rsem.at[6])

    for j in range(14):
        at = slice(j * 512, (j + 1) * 512)
        stream = gathered[s, :, at].astype(F32)
        mine = jnp.zeros((8, 512), F32)
        for t in range(4):
            mine = jnp.where(z == t, stream[t * 8 : t * 8 + 8], mine)
        if j < 8:
            moe = frecv[(j % 2) * 4 + j // 2, :, 0:512].astype(F32)[0:8]
        else:
            core, c = (j - 8) // 3, (j - 8) % 3
            moe = jnp.zeros((8, 512), F32)
            for t in range(4):
                piece = frecv[core * 4 + t, :, (0 if c == 1 else 512) : (512 if c == 1 else 1024)].astype(F32)
                moe = moe + (piece[0:8] if c == 0 else piece[8:16])
        attended[:, at] = mine.astype(BF)
        layer_out[:, at] = (mine + moe).astype(BF)

    for ref, number in (
        (route.at[pl.ds(0, 7)], 0),
        (picked.at[0, pl.ds(0, 31)], 1),
        (picked.at[pl.ds(1, 3), pl.ds(0, 31)], 2),
        (rows.at[:, pl.ds(0, 3072)], 3),
        (ysend.at[pl.ds(0, 3)], 4),
        (back.at[:, pl.ds(0, 31)], 5),
        (fsend.at[pl.ds(0, 7)], 6),
    ):
        wait(ref, ssem.at[number])


def expert_scratch():
    return [
        pltpu.VMEM((7168, 256), BF),
        pltpu.VMEM((7168, 256), BF),
        pltpu.VMEM((256, 7168), BF),
        pltpu.VMEM((8, 64, 128), BF),
        pltpu.VMEM((64, 7168), BF),
        pltpu.VMEM((512, 128), BF),
        pltpu.VMEM((4, 32, 16, 512), BF),
        pltpu.VMEM((256, 7168), BF),
        pltpu.VMEM((2, 256, 256), F32),
        pltpu.VMEM((256, 256), BF),
        pltpu.VMEM((4, 256, 1024), BF),
        pltpu.VMEM((4, 256, 1024), BF),
        pltpu.VMEM((6, 256, 512), BF),
        pltpu.VMEM((2, 256, 512), BF),
        pltpu.VMEM((4, 32, 16, 512), BF),
        pltpu.VMEM((4, 64, 512), F32),
        pltpu.VMEM((8, 16, 1024), BF),
        pltpu.VMEM((8, 16, 1024), BF),
    ]


def expert_call(expert_ids, gates, replicas, gain, w_gate, w_up, w_down, gathered):
    return pl.pallas_call(
        expert_phase,
        out_shape=[jax.ShapeDtypeStruct((8, 7168), BF)] * 2,
        in_specs=[SMEM, SMEM, SMEM, VMEM, ANY, ANY, ANY, VMEM],
        out_specs=[VMEM, VMEM],
        scratch_shapes=expert_scratch() + [pltpu.SemaphoreType.DMA((n,)) for n in (3, 7, 7, 4, 4, 4)],
        compiler_params=pltpu.CompilerParams(has_side_effects=True, vmem_limit_bytes=56 * MB),
        name="experts",
    )(expert_ids, gates.astype(F32), replicas, gain[None], w_gate[0], w_up[0], w_down[0], gathered)


def local(
    queries, cache, lengths, w_uv, w_out, resid, norm_gain, expert_ids, gate_weights, replica_slot, w_gate, w_up, w_down
):
    gathered = attention_call(lengths, queries, cache, w_uv, w_out, resid)
    return tuple(
        expert_call(expert_ids, gate_weights, replica_slot, norm_gain, w_gate, w_up, w_down, gathered)
    )


def solution(mesh):
    return jax.shard_map(
        local,
        mesh=mesh,
        in_specs=(
            P(("side", "dev"), None, None),
            P(("side", "dev"), None, None),
            P(("side", "dev")),
            P(("side", "dev"), None, None),
            P(("side", "dev"), None),
            P(("side", "dev"), None),
            P(),
            P(("side", "dev"), None),
            P(("side", "dev"), None),
            P(),
            P(("side", "dev"), None, None),
            P(("side", "dev"), None, None),
            P(("side", "dev"), None, None),
        ),
        out_specs=(P(("side", "dev"), None), P(("side", "dev"), None)),
        check_vma=False,
    )
```

time: 946 us -> 188 us (0.20)
  waiting for transfers between devices: 791 us -> 0 us
  Pallas kernels: 0 us -> 180 us
  matrix products: 38.6 us -> 0 us
  blocking collectives: 29 us -> 0 us
  starting transfers between devices: 25.6 us -> 0 us
  local copies, waits for them, and re-layouts: 29.1 us -> 6.57 us
  between operations: 14.3 us -> 0.65 us
  other arithmetic: 11.7 us -> 0.6 us
    reduce_scatter x1 -> x0, waiting for transfers between devices: 701 us -> none  [local(): lax.psum_scatter(jnp.dot(values, w_out, preferred_element_type=jnp.float3...]
    pallas_call x0 -> x2, Pallas kernels: none -> 180 us  [the longest x1 90.7 us: attention_call(): pl.pallas_call(attention_kernel, out_shape=jax.ShapeDtypeStruct((2, 32, 7...]
    all_to_all x3 -> x0, waiting for transfers between devices: 89.4 us -> none  [the longest x1 44.7 us: local(): lax.all_to_all(pieces, ('side', 'dev'), split_axis=0, concat_axis=0, tile...]
    dot_general x7 -> x0, matrix products: 38.6 us -> none  [the longest x1 12 us: local(): jnp.dot(values, w_out, preferred_element_type=jnp.float32)]
    all_to_all x1 -> x0, blocking collectives: 29 us -> none  [local(): lax.all_to_all(latent, ('side', 'dev'), split_axis=1, concat_axis=0, tile...]
    all_to_all x3 -> x0, starting transfers between devices: 25.5 us -> none  [the longest x1 14.7 us: local(): lax.all_to_all(pieces, ('side', 'dev'), split_axis=0, concat_axis=0, tile...]
    reshape x4 -> x0, local copies, waits for them, and re-layouts: 20.1 us -> none  [the longest x1 8.4 us: local(): flat_rows = rows_in.reshape(-1, width)]
    reduce_sum x6 -> x0, other arithmetic: 9.7 us -> none  [the longest x1 7.96 us: local(): jnp.sum(returned.reshape(slot_count, GROUP, capacity, width).astype(jnp.f...]
  transfers between devices with their start and end apart: 4 -> 0, of which waited for: 3 -> 0; matrix products, arithmetic and copies ran while one was open for 1% -> 0% of each run, Pallas kernels for 0% -> 0%
where the time goes in v1:
time: 188 us
  Pallas kernels  180 us (96%)
  local copies, waits for them, and re-layouts  6.57 us (3%)
    pallas_call x1, Pallas kernels, attention_call(): pl.pallas_call(attention_kernel, out_shape=jax.ShapeDtypeStruct((2, 32, 7...  90.7 us
    pallas_call x1, Pallas kernels, expert_call(): pl.pallas_call(expert_phase, out_shape=[jax.ShapeDtypeStruct((8, 7168), B...  89 us
    unnamed x5, local copies, waits for them, and re-layouts  6.57 us

profile of v1, /device:TPU:1, one launch (start us, length us, event | category | flops | bytes accessed | tf_op | source)
XLA Modules:
  0.0 187.6 jit_solution(2089240620462730217)
XLA Ops:
  0.6 0.8 copy.15
  1.4 0.6 convert_element_type.3.gates
  2.0 1.3 copy.16.expert_ids
  3.3 1.4 copy.17.replicas
  4.7 90.7 %attention.1.gathered = bf16[2,32,7168]{2,1,0:T(8,128)(2,1)} custom-call(s32[8]{0:T(128)} %lengths.1, bf16[8,576,128]{2,1,0:T(8,128)(2,1)} %bitcast.11, bf16[8,576,512]{2,1,0:T(8,128)(2,1)} %bitcast.7, bf16[512,128]{1,0:T(8,128)(2,1)} %bitcast.12, bf16[128,7168]{1,0:T(8,128)(2,1)} %w_out.1, bf16[8,7168]{1,0:T(8,128)(2,1)} %resid.1), custom_call_target="tpu_custom_call" | custom-call | tf_op jit(solution)/shard_map/attention/pallas_call | solution.py:213
  95.4 89.0 %experts.1 = (bf16[8,7168]{1,0:T(8,128)(2,1)}, bf16[8,7168]{1,0:T(8,128)(2,1)}) custom-call(s32[8,4]{1,0:T(8,128)} %copy.16.expert_ids, f32[8,4]{1,0:T(8,128)} %convert_element_type.3.gates, s32[24,2]{1,0:T(8,128)} %copy.17.replicas, f32[1,7168]{1,0:T(1,128)} %bitcast.13, bf16[7168,256]{1,0:T(8,128)(2,1)} %bitcast.8, bf16[7168,256]{1,0:T(8,128)(2,1)} %bitcast.9, ...), custom_call_target="tpu_custom_call" | custom-call | tf_op jit(solution)/shard_map/experts/pallas_call | solution.py:429
  184.5 1.6 copy.20
  186.0 1.6 copy.21

commit v2 on v0

v2 whole, which is shorter than its diff:
```python
import functools
import math

import jax
import jax.numpy as jnp
from jax import lax
from jax.experimental import pallas as pl
from jax.experimental.pallas import tpu as pltpu
from jax.sharding import PartitionSpec as P

GROUP = 4
BF = jnp.bfloat16
F32 = jnp.float32
MB = 1 << 20


def place():
    s = lax.axis_index("side")
    dev = lax.axis_index("dev")
    return s, dev // 4, dev % 4


def dot(a, b, dims=((1,), (0,))):
    return lax.dot_general(a, b, (dims, ((), ())), preferred_element_type=F32)


def around(yx, k):
    return ((yx // 4 + k // 4) % 4) * 4 + (yx % 4 + k % 4) % 4


def iota(shape, dim):
    return lax.broadcasted_iota(jnp.int32, shape, dim)


W_UV, W_OUT, RESID, UV_OVER, OUT_OVER, LATENT, VALUE, SUM, SLICE, ROWS_OVER, ROUTE, PICK, PICK_REST, GATHER, PIECE, BACK, RESULT, SUM_ON = range(18)
PARTS = (1, 4, 1, 1, 1, 1, 4, 4, 2, 2, 1, 2, 1, 8, 4, 4, 1, 4)
FIRST = tuple(sum(PARTS[:i]) for i in range(len(PARTS)))


def kernel(
    lengths, expert_ids, gates, replicas,
    queries, cache, w_uv, w_out, resid, gain, w_gate, w_up, w_down,
    both,
    cbuf, late, lrecv, wuv, wo, vals, osend, orecv, tsend, trecv, rsend, rrecv, gathered,
    wg, wu, wd, route, normed, select, picked, rest, rows, acc, hidden, ysend, yrecv, bsend, asend, back, part, fsend, frecv,
    csem, ssem, rsem,
):
    def send(src, dst, kind, number, s, yx, z):
        pltpu.make_async_remote_copy(
            src_ref=src,
            dst_ref=dst,
            send_sem=ssem.at[kind],
            recv_sem=rsem.at[FIRST[kind] + number],
            device_id=(s, yx * 4 + z),
            device_id_type=pl.DeviceIdType.MESH,
        ).start()

    def keep(src, dst, kind, number):
        pltpu.make_async_copy(src, dst, rsem.at[FIRST[kind] + number]).start()

    def wait(ref, kind, number):
        pltpu.make_async_copy(ref, ref, rsem.at[FIRST[kind] + number]).wait()

    def sent(ref, kind):
        pltpu.make_async_copy(ref, ref, ssem.at[kind]).wait()

    s, yx, z = place()
    y, x = yx // 4, yx % 4

    barrier = pltpu.get_barrier_semaphore()

    def greet(core, chip, level):
        pl.semaphore_signal(
            barrier, inc=1, device_id=(core, chip * 4 + level), device_id_type=pl.DeviceIdType.MESH
        )

    def greet_plane(k, carry):
        greet((s + k % 2) % 2, around(yx, k // 2), z)
        return carry

    def greet_line(k, carry):
        greet((s + k // 4) % 2, yx, (z + k % 4) % 4)
        return carry

    lax.fori_loop(1, 4, greet_line, 0)
    lax.fori_loop(5, 8, greet_line, 0)
    lax.fori_loop(1, 32, greet_plane, 0)

    for r in range(8):
        pltpu.make_async_copy(cache.at[r], cbuf.at[r], csem.at[r]).start()
    own_col = pl.multiple_of((s * 4 + z) * 128, 128)
    here = pl.ds(pl.multiple_of(z * 1792, 256), 1792)
    for q in range(4):
        rsend[q] = resid[:, q * 1792 : (q + 1) * 1792].astype(F32)
    pl.semaphore_wait(barrier, 37)

    keep(w_uv, wuv.at[:, pl.ds(own_col, 128)], W_UV, 0)
    keep(w_out.at[:, here], wo.at[pl.ds(own_col, 128)], W_OUT, z)
    for k in (1, 3, 2):
        send(w_uv, wuv.at[:, pl.ds(own_col, 128)], W_UV, 0, s, yx, (z + k) % 4)
    for k in (1, 3, 2):
        t = (z + k) % 4
        there = pl.ds(pl.multiple_of(t * 1792, 256), 1792)
        send(w_out.at[:, there], wo.at[pl.ds(own_col, 128)], W_OUT, z, s, yx, t)
    send(w_uv, wuv.at[:, pl.ds(own_col, 128)], UV_OVER, 0, 1 - s, yx, z)
    send(w_out.at[:, here], wo.at[pl.ds(own_col, 128)], OUT_OVER, 0, 1 - s, yx, z)
    keep(rsend.at[z], rrecv.at[z], RESID, 0)
    for k in (1, 3, 2):
        t = (z + k) % 4
        send(rsend.at[t], rrecv.at[z], RESID, 0, s, yx, t)

    row, col = iota((128, 128), 0), iota((128, 128), 1)
    head = ((row % 8) // 4) * 64 + (row // 8) * 4 + row % 4
    order = jnp.where(col == head, 1.0, 0.0).astype(BF)
    scale = 1.0 / math.sqrt(192)
    column = iota((128, 512), 1)

    def one(r):
        pltpu.make_async_copy(cache.at[r], cbuf.at[r], csem.at[r]).wait()
        q = dot(order, queries[r], ((1,), (1,))).astype(BF)
        scores = dot(q, cbuf[r]) * scale
        scores = jnp.where(column < lengths[r], scores, -1e30)
        weight = jnp.exp(scores - jnp.max(scores, axis=1, keepdims=True))
        total = jnp.sum(weight, axis=1, keepdims=True)
        latent = dot(weight.astype(BF), cbuf[r, 0:512], ((1,), (1,)))
        return (latent / total).reshape(16, 8, 512)

    def step(i, carry):
        late[i] = jnp.concatenate([one(2 * i), one(2 * i + 1)], axis=1).astype(BF)
        keep(late.at[i, yx], lrecv.at[yx, i], LATENT, 0)

        def out(k, carry):
            to = around(yx, k)
            send(late.at[i, to], lrecv.at[yx, i], LATENT, 0, s, to, z)
            return carry

        return lax.fori_loop(1, 16, out, carry)

    lax.fori_loop(0, 4, step, 0)

    pltpu.make_async_copy(w_gate, wg, csem.at[8]).start()
    pltpu.make_async_copy(w_up, wu, csem.at[9]).start()
    pltpu.make_async_copy(w_down, wd, csem.at[10]).start()
    slot_me = s * 16 + yx
    line_me = s * 4 + z

    half = pl.ds(pl.multiple_of(s * 512, 512), 512)
    wait(wuv.at[:, half], W_UV, 0)
    for k in (1, 3, 2):
        at = pl.ds(pl.multiple_of((s * 4 + (z + k) % 4) * 128, 128), 128)
        send(wuv.at[:, at], wuv.at[:, at], UV_OVER, 0, 1 - s, yx, z)

    row, lane = iota((64, 128), 0), iota((64, 128), 1)

    def choice(p, carry):
        table, used = carry
        t, k = p // 4, p % 4
        slot = replicas[(t + k) % 2, expert_ids[k, t]]
        same = row // 2 == slot
        hit = same & (row % 2 == used)
        table = jnp.where(hit & (lane == line_me * 8 + t), 1.0, table)
        table = jnp.where(hit & (lane == 64 + line_me * 8 + t), gates[k, t], table)
        return table, used + jnp.where(same, 1, 0)

    table, _ = lax.fori_loop(0, 32, choice, (jnp.zeros((64, 128), F32), jnp.zeros((64, 128), jnp.int32)))
    route[line_me] = table.astype(BF)

    def announce(k, carry):
        send(route.at[line_me], route.at[line_me], ROUTE, 0, (s + k // 4) % 2, yx, (z + k % 4) % 4)
        return carry

    lax.fori_loop(1, 8, announce, 0)
    wait(wuv.at[:, half], UV_OVER, 0)
    wait(lrecv, LATENT, 0)

    mine = iota((256, 1024), 0) % 8 == iota((256, 1024), 1) // 128
    pick = jnp.where(iota((32, 256), 1) // 8 == iota((32, 256), 0), 1.0, 0.0).astype(BF)

    def value(j, carry):
        some = lrecv[pl.ds(j * 4, 4)].reshape(256, 512)
        full = dot(some, wuv[...])
        own = jnp.where(mine, full, 0.0).astype(BF)
        vals[z, j] = dot(pick, own).astype(BF)
        for k in (1, 3, 2):
            send(vals.at[z, j], vals.at[z, j], VALUE, z, s, yx, (z + k) % 4)
        return carry

    lax.fori_loop(0, 4, value, 0)

    for k in (1, 3, 2, 0):
        t = (z + k) % 4
        at = pl.ds(pl.multiple_of((s * 4 + t) * 128, 128), 128)
        wait(wo.at[at], W_OUT, t)
        if k:
            send(wo.at[at], wo.at[at], OUT_OVER, 0, 1 - s, yx, z)

    wait(route.at[pl.ds(0, 7)], ROUTE, 0)
    a, b = iota((512, 512), 0), iota((512, 512), 1)
    deal = jnp.where(b == ((a % 16) // 2) * 64 + (a // 16) * 2 + a % 2, 1.0, 0.0).astype(BF)
    select[...] = dot(deal, route[...].reshape(512, 128)).astype(BF)
    wait(wo.at[half], OUT_OVER, 0)

    def of(ref, t, along):
        return ref.at[:, t, :, 0:896] if along == 0 else ref.at[t, :, :, 896:1792]

    def chip(t, along):
        return y * 4 + t if along == 0 else t * 4 + x

    place_on = (x, y)
    for pp in range(2):
        p = (z // 2 + pp) % 2
        for e in range(2):
            @pl.when(2 * p + e != z)
            def _():
                wait(vals.at[2 * p + e], VALUE, 2 * p + e)

        def project(c, carry):
            at = pl.ds(pl.multiple_of(c * 256, 256), 256)
            got = dot(vals[pl.ds(2 * p, 2)].reshape(256, 1024), wo[:, at]).reshape(2, 16, 8, 256)
            osend[p, :, :, :, at] = jnp.concatenate([got[0], got[1]], axis=1).astype(BF).reshape(4, 4, 16, 256)
            return carry

        lax.fori_loop(0, 7, project, 0)
        for along in range(2):
            at = place_on[along]
            keep(of(osend.at[p], at, along), orecv.at[p, along, at], SUM, 2 * p + along)
            for k in (1, 3, 2):
                t = (at + k) % 4
                send(of(osend.at[p], t, along), orecv.at[p, along, at], SUM, 2 * p + along, s, chip(t, along), z)

    for pp in range(2):
        p = (z // 2 + pp) % 2
        for along in range(2):
            wait(orecv.at[p, along], SUM, 2 * p + along)
            got = [orecv[p, along, i].astype(F32) for i in range(4)]
            tsend[p, along] = ((got[0] + got[1]) + (got[2] + got[3])).astype(BF)
            at = place_on[1 - along]
            keep(tsend.at[p, along, at], trecv.at[p, along, at], SUM_ON, 2 * p + along)
            for k in (1, 3, 2):
                t = (at + k) % 4
                send(
                    tsend.at[p, along, t], trecv.at[p, along, at],
                    SUM_ON, 2 * p + along, s, chip(t, 1 - along), z,
                )

    wait(rrecv, RESID, 0)
    for pp in range(2):
        p = (z // 2 + pp) % 2
        line = pl.ds(pl.multiple_of(p * 16, 16), 16)
        for along in range(2):
            wait(trecv.at[p, along], SUM_ON, 2 * p + along)
            got = [trecv[p, along, i].astype(F32) for i in range(4)]
            cols = slice(along * 896, along * 896 + 896)
            base = jnp.concatenate([rrecv[2 * p, :, cols], rrecv[2 * p + 1, :, cols]], axis=0)
            total = base + ((got[0] + got[1]) + (got[2] + got[3]))
            gathered[s, line, pl.ds(pl.multiple_of(z * 1792 + along * 896, 128), 896)] = total.astype(BF)
        for k in (1, 3, 2):
            send(gathered.at[s, line, here], gathered.at[s, line, here], SLICE, p, s, yx, (z + k) % 4)

    def norm(core, p):
        stream = gathered[core, pl.ds(pl.multiple_of(p * 16, 16), 16)].astype(F32)
        mean = jnp.mean(stream * stream, axis=1, keepdims=True)
        at = pl.ds(pl.multiple_of(core * 32 + p * 16, 16), 16)
        normed[at] = (stream * lax.rsqrt(mean + 1e-06) * gain[...]).astype(BF)

    for pp in range(2):
        p = (z // 2 + pp) % 2
        line = pl.ds(pl.multiple_of(p * 16, 16), 16)
        wait(gathered.at[s, line, pl.ds(0, 5376)], SLICE, p)
        send(gathered.at[s, line], gathered.at[s, line], ROWS_OVER, p, 1 - s, yx, z)
        norm(s, p)
    for pp in range(2):
        p = (z // 2 + pp) % 2
        wait(gathered.at[s, pl.ds(0, 16)], ROWS_OVER, p)
        norm(1 - s, p)

    land = pl.ds(pl.multiple_of(yx * 16, 16), 16)

    def deliver(source, cols, kind, number):
        keep(source.at[slot_me], rows.at[land, cols], kind, number)

        def out(k, carry):
            to, core = around(yx, k // 2), (s + k % 2) % 2
            send(source.at[core * 16 + to], rows.at[land, cols], kind, number, core, to, z)
            return carry

        lax.fori_loop(1, 32, out, 0)

    def deliver_slice(c):
        cols = pl.ds(pl.multiple_of(z * 1024 + c * 512 + s * 256, 256), 256)
        picked[c] = dot(select[:, 0:64], normed[:, cols]).astype(BF).reshape(32, 16, 256)
        deliver(picked.at[c], cols, PICK, c)

    def deliver_rest(c):
        cols = pl.ds(pl.multiple_of(4096 + s * 1536 + c * 512, 512), 512)
        rest[c] = dot(select[:, 0:64], normed[:, cols]).astype(BF).reshape(32, 16, 512)
        deliver(rest.at[c], cols, PICK_REST, 0)

    def spread(c):
        cols = pl.ds(pl.multiple_of(z * 1024 + c * 512, 512), 512)
        wait(rows.at[:, cols], PICK, c)
        for k in (1, 3, 2):
            send(rows.at[:, cols], rows.at[:, cols], GATHER, c * 4 + z, s, yx, (z + k) % 4)

    deliver_slice(0)
    deliver_slice(1)
    deliver_rest(0)
    spread(0)
    deliver_rest(1)
    spread(1)
    deliver_rest(2)

    pltpu.make_async_copy(w_gate, wg, csem.at[8]).wait()
    pltpu.make_async_copy(w_up, wu, csem.at[9]).wait()
    acc[...] = jnp.zeros_like(acc)

    def enter(c, carry):
        at = pl.ds(pl.multiple_of(c * 512, 512), 512)
        acc[0] += dot(rows[:, at], wg[at])
        acc[1] += dot(rows[:, at], wu[at])
        return carry

    lax.fori_loop(2 * z, 2 * z + 2, enter, 0)
    for c in range(2):
        for k in (1, 3, 2):
            t = (z + k) % 4
            wait(rows.at[:, pl.ds(pl.multiple_of(t * 1024 + c * 512, 512), 512)], GATHER, c * 4 + t)
            enter(2 * t + c, 0)
    wait(rows.at[:, pl.ds(4096, 3072)], PICK_REST, 0)
    lax.fori_loop(8, 14, enter, 0)
    gate = acc[0]
    hidden[...] = (gate * jax.nn.sigmoid(gate) * acc[1]).astype(BF)
    pltpu.make_async_copy(w_down, wd, csem.at[10]).wait()

    for k in (1, 3, 2, 0):
        t = (z + k) % 4
        got = dot(hidden[...], wd[:, pl.ds(pl.multiple_of(t * 1024, 1024), 1024)]).astype(BF)
        if k == 0:
            yrecv[z] = got
        else:
            ysend[t] = got
    for j in range(4):
        some = pl.ds(pl.multiple_of(((y + j) % 4) * 64, 64), 64)
        for k in (1, 3, 2):
            t = (z + k) % 4
            send(ysend.at[t, some], yrecv.at[z, some], PIECE, (y + j) % 4, s, yx, t)

    def give(source, core, to, c):
        src = source.at[pl.ds(pl.multiple_of(to * 16, 16), 16)]
        send(src, back.at[c, slot_me], BACK, c, core, to, z)

    def give_own(source, core, c):
        @pl.when(core == s)
        def _():
            keep(source.at[land], back.at[c, slot_me], BACK, c)

        @pl.when(core != s)
        def _():
            give(source, core, yx, c)

    for c in range(3):
        for core in range(2):
            j = core * 3 + c
            bsend[j] = dot(hidden[...], wd[:, 4096 + j * 512 : 4608 + j * 512]).astype(BF)
            give_own(bsend.at[j], core, c)

            def out(k, carry):
                give(bsend.at[j], core, around(yx, k), c)
                return carry

            lax.fori_loop(1, 16, out, 0)

    for j in range(4):
        to_y = (y + j) % 4
        some = pl.ds(pl.multiple_of(to_y * 64, 64), 64)
        wait(yrecv.at[pl.ds(0, 3), some], PIECE, to_y)
        got = [yrecv[q, some].astype(F32) for q in range(4)]
        total = ((got[0] + got[1]) + (got[2] + got[3])).astype(BF)
        for core in range(2):
            asend[core, some] = total[:, core * 512 : core * 512 + 512]
            if j == 0:
                give_own(asend.at[core], core, 3)
            for k in range(1 if j == 0 else 0, 4):
                give(asend.at[core], core, to_y * 4 + (x + k) % 4, 3)

    for c in range(4):
        wait(back.at[c], BACK, c)
        part[c] = dot(select[...], back[c].reshape(512, 512), ((0,), (0,)))[64:128]

    def pair(c, d):
        return jnp.concatenate([part[c].reshape(8, 8, 512), part[d].reshape(8, 8, 512)], axis=1).astype(BF)

    fsend[:, :, 0:512] = pair(3, 1)
    fsend[:, :, 512:1024] = pair(0, 2)
    keep(fsend.at[line_me], frecv.at[line_me], RESULT, 0)

    def finish(k, carry):
        core, to = (s + k // 4) % 2, (z + k % 4) % 4
        send(fsend.at[core * 4 + to], frecv.at[line_me], RESULT, 0, core, yx, to)
        return carry

    lax.fori_loop(1, 8, finish, 0)
    wait(frecv, RESULT, 0)

    for j in range(14):
        at = slice(j * 512, (j + 1) * 512)
        stream = gathered[s, :, at].astype(F32)
        own = jnp.zeros((8, 512), F32)
        for t in range(4):
            own = jnp.where(z == t, stream[t * 8 : t * 8 + 8], own)
        if j < 8:
            moe = frecv[(j % 2) * 4 + j // 2, :, 0:512].astype(F32)[0:8]
        else:
            core, c = (j - 8) // 3, (j - 8) % 3
            moe = jnp.zeros((8, 512), F32)
            for t in range(4):
                piece = frecv[core * 4 + t, :, (0 if c == 1 else 512) : (512 if c == 1 else 1024)].astype(F32)
                moe = moe + (piece[0:8] if c == 0 else piece[8:16])
        both[0, :, at] = own.astype(BF)
        both[1, :, at] = (own + moe).astype(BF)

    for ref, kind in (
        (wuv.at[:, pl.ds(0, 384)], W_UV),
        (wo.at[pl.ds(0, 384)], W_OUT),
        (rsend.at[pl.ds(0, 3)], RESID),
        (wuv.at[:, half], UV_OVER),
        (wo.at[half], OUT_OVER),
        (late.at[:, pl.ds(0, 15)], LATENT),
        (vals.at[pl.ds(0, 3)], VALUE),
        (orecv.at[:, :, pl.ds(0, 3)], SUM),
        (tsend.at[:, :, pl.ds(0, 3)], SUM_ON),
        (gathered.at[s, :, pl.ds(0, 5376)], SLICE),
        (gathered.at[s], ROWS_OVER),
        (route.at[pl.ds(0, 7)], ROUTE),
        (picked.at[:, pl.ds(0, 31)], PICK),
        (rest.at[:, pl.ds(0, 31)], PICK_REST),
        (rows.at[:, pl.ds(0, 3072)], GATHER),
        (ysend.at[pl.ds(0, 3)], PIECE),
        (back.at[:, pl.ds(0, 31)], BACK),
        (fsend.at[pl.ds(0, 7)], RESULT),
    ):
        sent(ref, kind)


VMEM = pl.BlockSpec(memory_space=pltpu.VMEM)
SMEM = pl.BlockSpec(memory_space=pltpu.SMEM)
ANY = pl.BlockSpec(memory_space=pl.ANY)


def local(
    queries, cache, lengths, w_uv, w_out, resid, norm_gain, expert_ids, gate_weights, replica_slot, w_gate, w_up, w_down
):
    scratch = [
        pltpu.VMEM((8, 576, 512), BF),
        pltpu.VMEM((4, 16, 16, 512), BF),
        pltpu.VMEM((16, 4, 16, 512), BF),
        pltpu.VMEM((512, 1024), BF),
        pltpu.VMEM((1024, 1792), BF),
        pltpu.VMEM((4, 4, 32, 1024), BF),
        pltpu.VMEM((2, 4, 4, 16, 1792), BF),
        pltpu.VMEM((2, 2, 4, 4, 16, 896), BF),
        pltpu.VMEM((2, 2, 4, 16, 896), BF),
        pltpu.VMEM((2, 2, 4, 16, 896), BF),
        pltpu.VMEM((4, 8, 1792), F32),
        pltpu.VMEM((4, 8, 1792), F32),
        pltpu.VMEM((2, 32, 7168), BF),
        pltpu.VMEM((7168, 256), BF),
        pltpu.VMEM((7168, 256), BF),
        pltpu.VMEM((256, 7168), BF),
        pltpu.VMEM((8, 64, 128), BF),
        pltpu.VMEM((64, 7168), BF),
        pltpu.VMEM((512, 128), BF),
        pltpu.VMEM((2, 32, 16, 256), BF),
        pltpu.VMEM((3, 32, 16, 512), BF),
        pltpu.VMEM((256, 7168), BF),
        pltpu.VMEM((2, 256, 256), F32),
        pltpu.VMEM((256, 256), BF),
        pltpu.VMEM((4, 256, 1024), BF),
        pltpu.VMEM((4, 256, 1024), BF),
        pltpu.VMEM((6, 256, 512), BF),
        pltpu.VMEM((2, 256, 512), BF),
        pltpu.VMEM((4, 32, 16, 512), BF),
        pltpu.VMEM((4, 64, 512), F32),
        pltpu.VMEM((8, 16, 1024), BF),
        pltpu.VMEM((8, 16, 1024), BF),
    ] + [pltpu.SemaphoreType.DMA((n,)) for n in (11, len(PARTS), sum(PARTS))]
    both = pl.pallas_call(
        kernel,
        out_shape=jax.ShapeDtypeStruct((2, 8, 7168), BF),
        in_specs=[SMEM] * 4 + [VMEM, ANY, ANY, ANY, VMEM, VMEM, ANY, ANY, ANY],
        out_specs=VMEM,
        scratch_shapes=scratch,
        compiler_params=pltpu.CompilerParams(collective_id=0, has_side_effects=True, vmem_limit_bytes=60 * MB),
        name="layer",
    )(
        lengths,
        expert_ids.T,
        gate_weights.T.astype(F32),
        replica_slot.T,
        jnp.swapaxes(queries, 1, 2),
        jnp.swapaxes(cache, 1, 2),
        w_uv[0],
        w_out,
        resid,
        norm_gain[None],
        w_gate[0],
        w_up[0],
        w_down[0],
    )
    return both[0], both[1]


def solution(mesh):
    return jax.shard_map(
        local,
        mesh=mesh,
        in_specs=(
            P(("side", "dev"), None, None),
            P(("side", "dev"), None, None),
            P(("side", "dev")),
            P(("side", "dev"), None, None),
            P(("side", "dev"), None),
            P(("side", "dev"), None),
            P(),
            P(("side", "dev"), None),
            P(("side", "dev"), None),
            P(),
            P(("side", "dev"), None, None),
            P(("side", "dev"), None, None),
            P(("side", "dev"), None, None),
        ),
        out_specs=(P(("side", "dev"), None), P(("side", "dev"), None)),
        check_vma=False,
    )
```

time: 946 us -> 150 us (0.16)
  waiting for transfers between devices: 791 us -> 0 us
  Pallas kernels: 0 us -> 146 us
  matrix products: 38.6 us -> 0 us
  blocking collectives: 29 us -> 0 us
  local copies, waits for them, and re-layouts: 29.1 us -> 1.65 us
  starting transfers between devices: 25.6 us -> 0 us
  between operations: 14.3 us -> 0.64 us
  other arithmetic: 11.7 us -> 1.26 us
    reduce_scatter x1 -> x0, waiting for transfers between devices: 701 us -> none  [local(): lax.psum_scatter(jnp.dot(values, w_out, preferred_element_type=jnp.float3...]
    pallas_call x0 -> x1, Pallas kernels: none -> 146 us  [local(): pl.pallas_call(kernel, out_shape=jax.ShapeDtypeStruct((2, 8, 7168), BF),...]
    all_to_all x3 -> x0, waiting for transfers between devices: 89.4 us -> none  [the longest x1 44.7 us: local(): lax.all_to_all(pieces, ('side', 'dev'), split_axis=0, concat_axis=0, tile...]
    dot_general x7 -> x0, matrix products: 38.6 us -> none  [the longest x1 12 us: local(): jnp.dot(values, w_out, preferred_element_type=jnp.float32)]
    all_to_all x1 -> x0, blocking collectives: 29 us -> none  [local(): lax.all_to_all(latent, ('side', 'dev'), split_axis=1, concat_axis=0, tile...]
    all_to_all x3 -> x0, starting transfers between devices: 25.5 us -> none  [the longest x1 14.7 us: local(): lax.all_to_all(pieces, ('side', 'dev'), split_axis=0, concat_axis=0, tile...]
    reshape x4 -> x0, local copies, waits for them, and re-layouts: 20.1 us -> none  [the longest x1 8.4 us: local(): flat_rows = rows_in.reshape(-1, width)]
    reduce_sum x6 -> x0, other arithmetic: 9.7 us -> none  [the longest x1 7.96 us: local(): jnp.sum(returned.reshape(slot_count, GROUP, capacity, width).astype(jnp.f...]
  transfers between devices with their start and end apart: 4 -> 0, of which waited for: 3 -> 0; matrix products, arithmetic and copies ran while one was open for 1% -> 0% of each run, Pallas kernels for 0% -> 0%
where the time goes in v2:
time: 150 us
  Pallas kernels  146 us (97%)
  local copies, waits for them, and re-layouts  1.65 us (1%)
    pallas_call x1, Pallas kernels, local(): pl.pallas_call(kernel, out_shape=jax.ShapeDtypeStruct((2, 8, 7168), BF),...  146 us

profile of v2, /device:TPU:1, one launch (start us, length us, event | category | flops | bytes accessed | tf_op | source)
XLA Modules:
  0.0 149.7 jit_solution(9466393065554194801)
XLA Ops:
  0.6 1.3 convert_bitcast_fusion.gates
  1.9 146.2 %layer.1 = bf16[2,8,7168]{2,1,0:T(8,128)(2,1)} custom-call(s32[8]{0:T(128)} %lengths.1, s32[4,8]{1,0:T(4,128)} %bitcast.22, f32[4,8]{1,0:T(4,128)} %convert_bitcast_fusion.gates, s32[2,24]{1,0:T(2,128)} %bitcast.23, bf16[8,576,128]{2,1,0:T(8,128)(2,1)} %bitcast.19, bf16[8,576,512]{2,1,0:T(8,128)(2,1)} %bitcast.15, bf16[512,128]{1,0:T(8,128)(2,1)} %bitcast.20, ...), custom_call_target="tpu_custom_call" | custom-call | tf_op jit(solution)/shard_map/layer/pallas_call | solution.py:487
  148.1 1.7 %slice_bitcast_fusion = (bf16[8,7168]{1,0:T(8,128)(2,1)}, bf16[8,7168]{1,0:T(8,128)(2,1)}) fusion(bf16[2,8,7168]{2,1,0:T(8,128)(2,1)} %layer.1), kind=kLoop, calls=%fused_computation | loop fusion | bytes 458752 | tf_op jit(solution)/shard_map/squeeze | solution.py:510

commit v3 on v2

--- a/solution.py
+++ b/solution.py
@@ -32,8 +32,8 @@
     return lax.broadcasted_iota(jnp.int32, shape, dim)
 
 
-W_UV, W_OUT, RESID, UV_OVER, OUT_OVER, LATENT, VALUE, SUM, SLICE, ROWS_OVER, ROUTE, PICK, PICK_REST, GATHER, PIECE, BACK, RESULT, SUM_ON = range(18)
-PARTS = (1, 4, 1, 1, 1, 1, 4, 4, 2, 2, 1, 2, 1, 8, 4, 4, 1, 4)
+W_UV, W_OUT, RESID, UV_OVER, OUT_OVER, LATENT, VALUE, SUM, SLICE, ROWS_OVER, ROUTE, PICK, PICK_REST, GATHER, PIECE, BACK, RESULT, SUM_ON, TABLE, LINES, HOME, HOME_ON = range(22)
+PARTS = (1, 4, 1, 1, 1, 1, 4, 4, 2, 2, 1, 2, 4, 8, 4, 1, 1, 4, 2, 4, 4, 4)
 FIRST = tuple(sum(PARTS[:i]) for i in range(len(PARTS)))
 
 
@@ -42,7 +42,8 @@
     queries, cache, w_uv, w_out, resid, gain, w_gate, w_up, w_down,
     both,
     cbuf, late, lrecv, wuv, wo, vals, osend, orecv, tsend, trecv, rsend, rrecv, gathered,
-    wg, wu, wd, route, normed, select, picked, rest, rows, acc, hidden, ysend, yrecv, bsend, asend, back, part, fsend, frecv,
+    wg, wu, wd, route, normed, select, tables, picked, picked_on, lines, rest, rows, acc, hidden,
+    ysend, yrecv, bsend, brecv, tsend_home, trecv_home, asend, back, fsend, frecv,
     csem, ssem, rsem,
 ):
     def send(src, dst, kind, number, s, yx, z):
@@ -197,7 +198,18 @@
     wait(route.at[pl.ds(0, 7)], ROUTE, 0)
     a, b = iota((512, 512), 0), iota((512, 512), 1)
     deal = jnp.where(b == ((a % 16) // 2) * 64 + (a // 16) * 2 + a % 2, 1.0, 0.0).astype(BF)
-    select[...] = dot(deal, route[...].reshape(512, 128)).astype(BF)
+    select[...] = dot(deal, route[...].reshape(512, 128)).astype(BF).reshape(2, 4, 4, 16, 128)
+    for along in range(2):
+        at = (x, y)[along]
+
+        def column(t):
+            return select.at[:, :, t] if along == 0 else select.at[:, t]
+
+        keep(column(at), tables.at[along, at], TABLE, along)
+        for k in (1, 3, 2):
+            t = (at + k) % 4
+            to = y * 4 + t if along == 0 else t * 4 + x
+            send(column(t), tables.at[along, at], TABLE, along, s, to, z)
     wait(wo.at[half], OUT_OVER, 0)
 
     def of(ref, t, along):
@@ -275,66 +287,101 @@
         norm(1 - s, p)
 
     land = pl.ds(pl.multiple_of(yx * 16, 16), 16)
-
-    def deliver(source, cols, kind, number):
-        keep(source.at[slot_me], rows.at[land, cols], kind, number)
+    flat = select[...].reshape(512, 128)[:, 0:64]
+
+    def slice_cols(t, c, core):
+        start, width = ((0, 128), (256, 256))[c]
+        return pl.ds(pl.multiple_of(t * 768 + start + core * width, 128), width)
+
+    def whole_cols(t, c):
+        start, width = ((0, 256), (256, 512))[c]
+        return pl.ds(pl.multiple_of(t * 768 + start, 256), width)
+
+    def rest_cols(core, along, c):
+        return pl.ds(pl.multiple_of(3072 + core * 2048 + along * 1024 + c * 512, 512), 512)
+
+    def deliver_slice(c, buffer):
+        cols = slice_cols(z, c, s)
+        width = (128, 256)[c]
+        buffer[...] = dot(flat, normed[:, cols]).astype(BF).reshape(32, 16, width)
+        place_in = rows.at[y, x, :, cols]
+        keep(buffer.at[slot_me], place_in, PICK, c)
 
         def out(k, carry):
             to, core = around(yx, k // 2), (s + k % 2) % 2
-            send(source.at[core * 16 + to], rows.at[land, cols], kind, number, core, to, z)
+            send(buffer.at[core * 16 + to], place_in, PICK, c, core, to, z)
             return carry
 
         lax.fori_loop(1, 32, out, 0)
 
-    def deliver_slice(c):
-        cols = pl.ds(pl.multiple_of(z * 1024 + c * 512 + s * 256, 256), 256)
-        picked[c] = dot(select[:, 0:64], normed[:, cols]).astype(BF).reshape(32, 16, 256)
-        deliver(picked.at[c], cols, PICK, c)
+    def share_lines(c):
+        for along in range(2):
+            at = place_on[along]
+            source = normed.at[:, rest_cols(s, along, c)]
+            keep(source, lines.at[along, c, at], LINES, 2 * along + c)
+            for k in (1, 3, 2):
+                send(source, lines.at[along, c, at], LINES, 2 * along + c, s, chip((at + k) % 4, along), z)
 
     def deliver_rest(c):
-        cols = pl.ds(pl.multiple_of(4096 + s * 1536 + c * 512, 512), 512)
-        rest[c] = dot(select[:, 0:64], normed[:, cols]).astype(BF).reshape(32, 16, 512)
-        deliver(rest.at[c], cols, PICK_REST, 0)
+        for along in range(2):
+            wait(lines.at[along, c], LINES, 2 * along + c)
+            for t in range(4):
+                table = tables[along, t].reshape(128, 128)[:, 0:64]
+                rest[along, c, :, :, t] = dot(table, lines[along, c, t]).astype(BF).reshape(2, 4, 16, 512)
+            cols = rest_cols(s, along, c)
+            place_in = rows.at[y, :, :, cols] if along == 0 else rows.at[:, x, :, cols]
+            at = place_on[1 - along]
+            keep(rest.at[along, c, s, at], place_in, PICK_REST, 2 * along + c)
+            for k in (1, 3, 2):
+                t = (at + k) % 4
+                for core in range(2):
+                    send(rest.at[along, c, core, t], place_in, PICK_REST, 2 * along + c, core, chip(t, 1 - along), z)
+            send(rest.at[along, c, 1 - s, at], place_in, PICK_REST, 2 * along + c, 1 - s, yx, z)
 
     def spread(c):
-        cols = pl.ds(pl.multiple_of(z * 1024 + c * 512, 512), 512)
-        wait(rows.at[:, cols], PICK, c)
+        cols = whole_cols(z, c)
+        wait(rows.at[:, :, :, cols], PICK, c)
         for k in (1, 3, 2):
-            send(rows.at[:, cols], rows.at[:, cols], GATHER, c * 4 + z, s, yx, (z + k) % 4)
-
-    deliver_slice(0)
-    deliver_slice(1)
+            send(rows.at[:, :, :, cols], rows.at[:, :, :, cols], GATHER, c * 4 + z, s, yx, (z + k) % 4)
+
+    wait(tables.at[0], TABLE, 0)
+    wait(tables.at[1], TABLE, 1)
+    deliver_slice(0, picked)
+    share_lines(0)
+    deliver_slice(1, picked_on)
+    share_lines(1)
+    spread(0)
     deliver_rest(0)
-    spread(0)
+    spread(1)
     deliver_rest(1)
-    spread(1)
-    deliver_rest(2)
 
     pltpu.make_async_copy(w_gate, wg, csem.at[8]).wait()
     pltpu.make_async_copy(w_up, wu, csem.at[9]).wait()
     acc[...] = jnp.zeros_like(acc)
 
-    def enter(c, carry):
-        at = pl.ds(pl.multiple_of(c * 512, 512), 512)
-        acc[0] += dot(rows[:, at], wg[at])
-        acc[1] += dot(rows[:, at], wu[at])
-        return carry
-
-    lax.fori_loop(2 * z, 2 * z + 2, enter, 0)
+    def enter(at):
+        some = rows[:, :, :, at].reshape(256, at.size)
+        acc[0] += dot(some, wg[at])
+        acc[1] += dot(some, wu[at])
+
+    enter(whole_cols(z, 0))
+    enter(whole_cols(z, 1))
     for c in range(2):
         for k in (1, 3, 2):
             t = (z + k) % 4
-            wait(rows.at[:, pl.ds(pl.multiple_of(t * 1024 + c * 512, 512), 512)], GATHER, c * 4 + t)
-            enter(2 * t + c, 0)
-    wait(rows.at[:, pl.ds(4096, 3072)], PICK_REST, 0)
-    lax.fori_loop(8, 14, enter, 0)
+            wait(rows.at[:, :, :, whole_cols(t, c)], GATHER, c * 4 + t)
+            enter(whole_cols(t, c))
+        for along in range(2):
+            wait(rows.at[:, :, :, pl.ds(0, 1024)], PICK_REST, 2 * along + c)
+            for core in range(2):
+                enter(rest_cols(core, along, c))
     gate = acc[0]
     hidden[...] = (gate * jax.nn.sigmoid(gate) * acc[1]).astype(BF)
     pltpu.make_async_copy(w_down, wd, csem.at[10]).wait()
 
     for k in (1, 3, 2, 0):
         t = (z + k) % 4
-        got = dot(hidden[...], wd[:, pl.ds(pl.multiple_of(t * 1024, 1024), 1024)]).astype(BF)
+        got = dot(hidden[...], wd[:, pl.ds(pl.multiple_of(t * 768, 256), 768)]).astype(BF)
         if k == 0:
             yrecv[z] = got
         else:
@@ -345,53 +392,82 @@
             t = (z + k) % 4
             send(ysend.at[t, some], yrecv.at[z, some], PIECE, (y + j) % 4, s, yx, t)
 
-    def give(source, core, to, c):
-        src = source.at[pl.ds(pl.multiple_of(to * 16, 16), 16)]
-        send(src, back.at[c, slot_me], BACK, c, core, to, z)
-
-    def give_own(source, core, c):
-        @pl.when(core == s)
-        def _():
-            keep(source.at[land], back.at[c, slot_me], BACK, c)
-
-        @pl.when(core != s)
-        def _():
-            give(source, core, yx, c)
-
-    for c in range(3):
-        for core in range(2):
-            j = core * 3 + c
-            bsend[j] = dot(hidden[...], wd[:, 4096 + j * 512 : 4608 + j * 512]).astype(BF)
-            give_own(bsend.at[j], core, c)
-
-            def out(k, carry):
-                give(bsend.at[j], core, around(yx, k), c)
-                return carry
-
-            lax.fori_loop(1, 16, out, 0)
-
-    for j in range(4):
+    for c in range(2):
+        for along in range(2):
+            at = place_on[1 - along]
+
+            def part_of(core, t):
+                source = bsend.at[core, along, c]
+                return source.at[t] if along == 0 else source.at[:, t]
+
+            for core in range(2):
+                got = dot(hidden[...], wd[:, 3072 + core * 2048 + along * 1024 + c * 512 :][:, 0:512])
+                bsend[core, along, c] = got.astype(BF).reshape(4, 4, 16, 512)
+            land_in = brecv.at[along, c, s, at]
+            keep(part_of(s, at), land_in, HOME, 2 * along + c)
+            for k in (1, 3, 2):
+                t = (at + k) % 4
+                for core in range(2):
+                    send(part_of(core, t), land_in, HOME, 2 * along + c, core, chip(t, 1 - along), z)
+            send(part_of(1 - s, at), land_in, HOME, 2 * along + c, 1 - s, yx, z)
+
+    def give(core, to):
+        src = asend.at[core, pl.ds(pl.multiple_of(to * 16, 16), 16)]
+        send(src, back.at[slot_me], BACK, 0, core, to, z)
+
+    def home(c):
+        for along in range(2):
+            wait(brecv.at[along, c], HOME, 2 * along + c)
+            for t in range(4):
+                got = brecv[along, c, :, :, t].reshape(128, 512)
+                summed = dot(tables[along, t].reshape(128, 128), got, ((0,), (0,)))[64:128]
+                tsend_home[along, c, t] = summed.astype(BF)
+            at = place_on[along]
+            keep(tsend_home.at[along, c, at], trecv_home.at[along, c, at], HOME_ON, 2 * along + c)
+            for k in (1, 3, 2):
+                t = (at + k) % 4
+                send(
+                    tsend_home.at[along, c, t], trecv_home.at[along, c, at],
+                    HOME_ON, 2 * along + c, s, chip(t, along), z,
+                )
+
+    def slices(j):
         to_y = (y + j) % 4
         some = pl.ds(pl.multiple_of(to_y * 64, 64), 64)
         wait(yrecv.at[pl.ds(0, 3), some], PIECE, to_y)
         got = [yrecv[q, some].astype(F32) for q in range(4)]
         total = ((got[0] + got[1]) + (got[2] + got[3])).astype(BF)
         for core in range(2):
-            asend[core, some] = total[:, core * 512 : core * 512 + 512]
-            if j == 0:
-                give_own(asend.at[core], core, 3)
+            asend[core, some] = total[:, core * 384 : core * 384 + 384]
+        if j == 0:
+            keep(asend.at[s, land], back.at[slot_me], BACK, 0)
+            give(1 - s, yx)
+        for core in range(2):
             for k in range(1 if j == 0 else 0, 4):
-                give(asend.at[core], core, to_y * 4 + (x + k) % 4, 3)
-
-    for c in range(4):
-        wait(back.at[c], BACK, c)
-        part[c] = dot(select[...], back[c].reshape(512, 512), ((0,), (0,)))[64:128]
-
-    def pair(c, d):
-        return jnp.concatenate([part[c].reshape(8, 8, 512), part[d].reshape(8, 8, 512)], axis=1).astype(BF)
-
-    fsend[:, :, 0:512] = pair(3, 1)
-    fsend[:, :, 512:1024] = pair(0, 2)
+                give(core, to_y * 4 + (x + k) % 4)
+
+    slices(0)
+    home(0)
+    slices(1)
+    slices(2)
+    home(1)
+    slices(3)
+
+    for c in range(2):
+        for along in range(2):
+            wait(trecv_home.at[along, c], HOME_ON, 2 * along + c)
+            got = [trecv_home[along, c, i].astype(F32) for i in range(4)]
+            total = (got[0] + got[1]) + (got[2] + got[3])
+            if along == 0:
+                first = total
+            else:
+                both_rows = jnp.concatenate([first.reshape(8, 8, 512), total.reshape(8, 8, 512)], axis=1)
+                fsend[:, :, c * 512 : c * 512 + 512] = both_rows.astype(BF)
+    wait(back, BACK, 0)
+    total = dot(select[...].reshape(512, 128), back[...].reshape(512, 384), ((0,), (0,)))[64:128]
+    low = total[:, 0:256].reshape(8, 8, 256)
+    high = jnp.concatenate([total[:, 256:384], jnp.zeros((64, 128), F32)], axis=1).reshape(8, 8, 256)
+    fsend[:, :, 1024:1280] = jnp.concatenate([low, high], axis=1).astype(BF)
     keep(fsend.at[line_me], frecv.at[line_me], RESULT, 0)
 
     def finish(k, carry):
@@ -402,22 +478,25 @@
     lax.fori_loop(1, 8, finish, 0)
     wait(frecv, RESULT, 0)
 
-    for j in range(14):
-        at = slice(j * 512, (j + 1) * 512)
+    def write(first, width, moe):
+        at = slice(first, first + width)
         stream = gathered[s, :, at].astype(F32)
-        own = jnp.zeros((8, 512), F32)
+        own = jnp.zeros((8, width), F32)
         for t in range(4):
             own = jnp.where(z == t, stream[t * 8 : t * 8 + 8], own)
-        if j < 8:
-            moe = frecv[(j % 2) * 4 + j // 2, :, 0:512].astype(F32)[0:8]
-        else:
-            core, c = (j - 8) // 3, (j - 8) % 3
-            moe = jnp.zeros((8, 512), F32)
-            for t in range(4):
-                piece = frecv[core * 4 + t, :, (0 if c == 1 else 512) : (512 if c == 1 else 1024)].astype(F32)
-                moe = moe + (piece[0:8] if c == 0 else piece[8:16])
         both[0, :, at] = own.astype(BF)
         both[1, :, at] = (own + moe).astype(BF)
+
+    for j in range(8):
+        got = frecv[(j % 2) * 4 + j // 2, :, 1024:1280].astype(F32)
+        write(j * 384, 256, got[0:8])
+        write(j * 384 + 256, 128, got[8:16, 0:128])
+    for core in range(2):
+        for c in range(2):
+            got = [frecv[core * 4 + t, :, c * 512 : c * 512 + 512].astype(F32) for t in range(4)]
+            total = (got[0] + got[1]) + (got[2] + got[3])
+            write(3072 + core * 2048 + c * 512, 512, total[0:8])
+            write(3072 + core * 2048 + 1024 + c * 512, 512, total[8:16])
 
     for ref, kind in (
         (wuv.at[:, pl.ds(0, 384)], W_UV),
@@ -432,11 +511,18 @@
         (gathered.at[s, :, pl.ds(0, 5376)], SLICE),
         (gathered.at[s], ROWS_OVER),
         (route.at[pl.ds(0, 7)], ROUTE),
-        (picked.at[:, pl.ds(0, 31)], PICK),
-        (rest.at[:, pl.ds(0, 31)], PICK_REST),
-        (rows.at[:, pl.ds(0, 3072)], GATHER),
+        (tables.at[:, pl.ds(0, 3)], TABLE),
+        (picked.at[pl.ds(0, 31)], PICK),
+        (picked_on.at[pl.ds(0, 31)], PICK),
+        (lines.at[:, :, pl.ds(0, 3)], LINES),
+        (rest.at[:, :, 0], PICK_REST),
+        (rest.at[:, :, 1, pl.ds(0, 3)], PICK_REST),
+        (rows.at[:, :, :, pl.ds(0, 2304)], GATHER),
         (ysend.at[pl.ds(0, 3)], PIECE),
-        (back.at[:, pl.ds(0, 31)], BACK),
+        (back.at[pl.ds(0, 31)], BACK),
+        (brecv.at[:, :, 0], HOME),
+        (brecv.at[:, :, 1, pl.ds(0, 3)], HOME),
+        (tsend_home.at[:, :, pl.ds(0, 3)], HOME_ON),
         (fsend.at[pl.ds(0, 7)], RESULT),
     ):
         sent(ref, kind)
@@ -469,20 +555,25 @@
         pltpu.VMEM((256, 7168), BF),
         pltpu.VMEM((8, 64, 128), BF),
         pltpu.VMEM((64, 7168), BF),
-        pltpu.VMEM((512, 128), BF),
-        pltpu.VMEM((2, 32, 16, 256), BF),
-        pltpu.VMEM((3, 32, 16, 512), BF),
-        pltpu.VMEM((256, 7168), BF),
+        pltpu.VMEM((2, 4, 4, 16, 128), BF),
+        pltpu.VMEM((2, 4, 2, 4, 16, 128), BF),
+        pltpu.VMEM((32, 16, 128), BF),
+        pltpu.VMEM((32, 16, 256), BF),
+        pltpu.VMEM((2, 2, 4, 64, 512), BF),
+        pltpu.VMEM((2, 2, 2, 4, 4, 16, 512), BF),
+        pltpu.VMEM((4, 4, 16, 7168), BF),
         pltpu.VMEM((2, 256, 256), F32),
         pltpu.VMEM((256, 256), BF),
-        pltpu.VMEM((4, 256, 1024), BF),
-        pltpu.VMEM((4, 256, 1024), BF),
-        pltpu.VMEM((6, 256, 512), BF),
-        pltpu.VMEM((2, 256, 512), BF),
-        pltpu.VMEM((4, 32, 16, 512), BF),
-        pltpu.VMEM((4, 64, 512), F32),
-        pltpu.VMEM((8, 16, 1024), BF),
-        pltpu.VMEM((8, 16, 1024), BF),
+        pltpu.VMEM((4, 256, 768), BF),
+        pltpu.VMEM((4, 256, 768), BF),
+        pltpu.VMEM((2, 2, 2, 4, 4, 16, 512), BF),
+        pltpu.VMEM((2, 2, 2, 4, 4, 16, 512), BF),
+        pltpu.VMEM((2, 2, 4, 64, 512), BF),
+        pltpu.VMEM((2, 2, 4, 64, 512), BF),
+        pltpu.VMEM((2, 256, 384), BF),
+        pltpu.VMEM((32, 16, 384), BF),
+        pltpu.VMEM((8, 16, 1280), BF),
+        pltpu.VMEM((8, 16, 1280), BF),
     ] + [pltpu.SemaphoreType.DMA((n,)) for n in (11, len(PARTS), sum(PARTS))]
     both = pl.pallas_call(
         kernel,

time: 150 us -> 140 us (0.933)
  Pallas kernels: 146 us -> 136 us
    pallas_call x1, Pallas kernels: 146 us -> 136 us  [local(): pl.pallas_call(kernel, out_shape=jax.ShapeDtypeStruct((2, 8, 7168), BF),...]
where the time goes in v3:
time: 140 us
  Pallas kernels  136 us (97%)
  local copies, waits for them, and re-layouts  1.65 us (1%)
    pallas_call x1, Pallas kernels, local(): pl.pallas_call(kernel, out_shape=jax.ShapeDtypeStruct((2, 8, 7168), BF),...  136 us

profile of v3, /device:TPU:1, one launch (start us, length us, event | category | flops | bytes accessed | tf_op | source)
XLA Modules:
  0.0 139.9 jit_solution(7477267450153385664)
XLA Ops:
  0.6 1.3 convert_bitcast_fusion.gates
  1.9 136.4 %layer.1 = bf16[2,8,7168]{2,1,0:T(8,128)(2,1)} custom-call(s32[8]{0:T(128)} %lengths.1, s32[4,8]{1,0:T(4,128)} %bitcast.22, f32[4,8]{1,0:T(4,128)} %convert_bitcast_fusion.gates, s32[2,24]{1,0:T(2,128)} %bitcast.23, bf16[8,576,128]{2,1,0:T(8,128)(2,1)} %bitcast.19, bf16[8,576,512]{2,1,0:T(8,128)(2,1)} %bitcast.15, bf16[512,128]{1,0:T(8,128)(2,1)} %bitcast.20, ...), custom_call_target="tpu_custom_call" | custom-call | tf_op jit(solution)/shard_map/layer/pallas_call | solution.py:578
  138.3 1.7 %slice_bitcast_fusion = (bf16[8,7168]{1,0:T(8,128)(2,1)}, bf16[8,7168]{1,0:T(8,128)(2,1)}) fusion(bf16[2,8,7168]{2,1,0:T(8,128)(2,1)} %layer.1), kind=kLoop, calls=%fused_computation | loop fusion | bytes 458752 | tf_op jit(solution)/shard_map/squeeze | solution.py:601

commit v4 on v3

--- a/solution.py
+++ b/solution.py
@@ -33,7 +33,7 @@
 
 
 W_UV, W_OUT, RESID, UV_OVER, OUT_OVER, LATENT, VALUE, SUM, SLICE, ROWS_OVER, ROUTE, PICK, PICK_REST, GATHER, PIECE, BACK, RESULT, SUM_ON, TABLE, LINES, HOME, HOME_ON = range(22)
-PARTS = (1, 4, 1, 1, 1, 1, 4, 4, 2, 2, 1, 2, 4, 8, 4, 1, 1, 4, 2, 4, 4, 4)
+PARTS = (8, 8, 1, 1, 2, 1, 8, 8, 2, 2, 1, 2, 4, 8, 4, 1, 1, 8, 2, 4, 4, 4)
 FIRST = tuple(sum(PARTS[:i]) for i in range(len(PARTS)))
 
 
@@ -41,7 +41,7 @@
     lengths, expert_ids, gates, replicas,
     queries, cache, w_uv, w_out, resid, gain, w_gate, w_up, w_down,
     both,
-    cbuf, late, lrecv, wuv, wo, vals, osend, orecv, tsend, trecv, rsend, rrecv, gathered,
+    cbuf, qbuf, late, lrecv, wuv, wo, vals, osend, orecv, orecv_on, tsend, tsend_on, trecv, trecv_on, rsend, rrecv, gathered,
     wg, wu, wd, route, normed, select, tables, picked, picked_on, lines, rest, rows, acc, hidden,
     ysend, yrecv, bsend, brecv, tsend_home, trecv_home, asend, back, fsend, frecv,
     csem, ssem, rsem,
@@ -88,6 +88,7 @@
     lax.fori_loop(1, 32, greet_plane, 0)
 
     for r in range(8):
+        pltpu.make_async_copy(queries.at[r], qbuf.at[r], csem.at[11 + r]).start()
         pltpu.make_async_copy(cache.at[r], cbuf.at[r], csem.at[r]).start()
     own_col = pl.multiple_of((s * 4 + z) * 128, 128)
     here = pl.ds(pl.multiple_of(z * 1792, 256), 1792)
@@ -95,16 +96,41 @@
         rsend[q] = resid[:, q * 1792 : (q + 1) * 1792].astype(F32)
     pl.semaphore_wait(barrier, 37)
 
-    keep(w_uv, wuv.at[:, pl.ds(own_col, 128)], W_UV, 0)
-    keep(w_out.at[:, here], wo.at[pl.ds(own_col, 128)], W_OUT, z)
-    for k in (1, 3, 2):
-        send(w_uv, wuv.at[:, pl.ds(own_col, 128)], W_UV, 0, s, yx, (z + k) % 4)
-    for k in (1, 3, 2):
-        t = (z + k) % 4
-        there = pl.ds(pl.multiple_of(t * 1792, 256), 1792)
-        send(w_out.at[:, there], wo.at[pl.ds(own_col, 128)], W_OUT, z, s, yx, t)
+    def uv_part(t, h):
+        return wuv.at[pl.ds(h * 256, 256), pl.ds(pl.multiple_of((s * 4 + t) * 128, 128), 128)]
+
+    for h in range(2):
+        keep(w_uv.at[pl.ds(h * 256, 256)], uv_part(z, h), W_UV, 2 * z + h)
+        for k in (1, 3):
+            send(w_uv.at[pl.ds(h * 256, 256)], uv_part(z, h), W_UV, 2 * z + h, s, yx, (z + k) % 4)
+
+    parts = ((0, 1280), (1280, 512))
+
+    def out_part(t, c):
+        start, width = parts[c]
+        return w_out.at[:, pl.ds(pl.multiple_of(t * 1792 + start, 256), width)]
+
+    def wo_part(t, c):
+        start, width = parts[c]
+        return wo.at[pl.ds(pl.multiple_of((s * 4 + t) * 128, 128), 128), start : start + width]
+
+    def send_out(c):
+        for k in (1, 3, 2):
+            t = (z + k) % 4
+            send(out_part(t, c), wo_part(z, c), W_OUT, 2 * z + c, s, yx, t)
+
+    def pass_out(c):
+        for k in (1, 3, 2, 0):
+            t = (z + k) % 4
+            wait(wo_part(t, c), W_OUT, 2 * t + c)
+            if k:
+                send(wo_part(t, c), wo_part(t, c), OUT_OVER, c, 1 - s, yx, z)
+
+    send_out(0)
     send(w_uv, wuv.at[:, pl.ds(own_col, 128)], UV_OVER, 0, 1 - s, yx, z)
-    send(w_out.at[:, here], wo.at[pl.ds(own_col, 128)], OUT_OVER, 0, 1 - s, yx, z)
+    for c in range(2):
+        keep(out_part(z, c), wo_part(z, c), W_OUT, 2 * z + c)
+        send(out_part(z, c), wo_part(z, c), OUT_OVER, c, 1 - s, yx, z)
     keep(rsend.at[z], rrecv.at[z], RESID, 0)
     for k in (1, 3, 2):
         t = (z + k) % 4
@@ -117,8 +143,9 @@
     column = iota((128, 512), 1)
 
     def one(r):
+        pltpu.make_async_copy(queries.at[r], qbuf.at[r], csem.at[11 + r]).wait()
+        q = dot(order, qbuf[r], ((1,), (1,))).astype(BF)
         pltpu.make_async_copy(cache.at[r], cbuf.at[r], csem.at[r]).wait()
-        q = dot(order, queries[r], ((1,), (1,))).astype(BF)
         scores = dot(q, cbuf[r]) * scale
         scores = jnp.where(column < lengths[r], scores, -1e30)
         weight = jnp.exp(scores - jnp.max(scores, axis=1, keepdims=True))
@@ -137,7 +164,12 @@
 
         return lax.fori_loop(1, 16, out, carry)
 
-    lax.fori_loop(0, 4, step, 0)
+    step(0, 0)
+    for k, h in ((3, 0), (1, 1)):
+        t = (z + k) % 4
+        wait(uv_part(t, h), W_UV, 2 * t + h)
+        send(uv_part(t, h), uv_part(t, h), W_UV, 2 * t + h, s, yx, (z + 4 - k) % 4)
+    lax.fori_loop(1, 4, step, 0)
 
     pltpu.make_async_copy(w_gate, wg, csem.at[8]).start()
     pltpu.make_async_copy(w_up, wu, csem.at[9]).start()
@@ -146,24 +178,25 @@
     line_me = s * 4 + z
 
     half = pl.ds(pl.multiple_of(s * 512, 512), 512)
-    wait(wuv.at[:, half], W_UV, 0)
+    for k, h in ((0, 0), (0, 1), (3, 1), (1, 0), (2, 0), (2, 1)):
+        t = (z + k) % 4
+        wait(uv_part(t, h), W_UV, 2 * t + h)
     for k in (1, 3, 2):
         at = pl.ds(pl.multiple_of((s * 4 + (z + k) % 4) * 128, 128), 128)
         send(wuv.at[:, at], wuv.at[:, at], UV_OVER, 0, 1 - s, yx, z)
 
     row, lane = iota((64, 128), 0), iota((64, 128), 1)
 
-    def choice(p, carry):
-        table, used = carry
-        t, k = p // 4, p % 4
-        slot = replicas[(t + k) % 2, expert_ids[k, t]]
-        same = row // 2 == slot
-        hit = same & (row % 2 == used)
-        table = jnp.where(hit & (lane == line_me * 8 + t), 1.0, table)
-        table = jnp.where(hit & (lane == 64 + line_me * 8 + t), gates[k, t], table)
-        return table, used + jnp.where(same, 1, 0)
-
-    table, _ = lax.fori_loop(0, 32, choice, (jnp.zeros((64, 128), F32), jnp.zeros((64, 128), jnp.int32)))
+    gate_values = gates[...].astype(F32)
+    table, used = jnp.zeros((64, 128), F32), jnp.zeros((64, 128), jnp.int32)
+    for t in range(8):
+        for k in range(4):
+            slot = replicas[(t + k) % 2, expert_ids[k, t]]
+            same = row // 2 == slot
+            hit = same & (row % 2 == used)
+            table = jnp.where(hit & (lane == line_me * 8 + t), 1.0, table)
+            table = jnp.where(hit & (lane == 64 + line_me * 8 + t), gate_values[k : k + 1, t : t + 1], table)
+            used = used + jnp.where(same, 1, 0)
     route[line_me] = table.astype(BF)
 
     def announce(k, carry):
@@ -182,19 +215,22 @@
         full = dot(some, wuv[...])
         own = jnp.where(mine, full, 0.0).astype(BF)
         vals[z, j] = dot(pick, own).astype(BF)
-        for k in (1, 3, 2):
-            send(vals.at[z, j], vals.at[z, j], VALUE, z, s, yx, (z + k) % 4)
+        for k in (1, 3):
+            send(vals.at[z, j], vals.at[z, j], VALUE, 2 * z + j // 2, s, yx, (z + k) % 4)
         return carry
 
     lax.fori_loop(0, 4, value, 0)
 
-    for k in (1, 3, 2, 0):
+    def values_of(k, h):
         t = (z + k) % 4
-        at = pl.ds(pl.multiple_of((s * 4 + t) * 128, 128), 128)
-        wait(wo.at[at], W_OUT, t)
-        if k:
-            send(wo.at[at], wo.at[at], OUT_OVER, 0, 1 - s, yx, z)
-
+        wait(vals.at[t, pl.ds(2 * h, 2)], VALUE, 2 * t + h)
+        return vals.at[t, pl.ds(2 * h, 2)], 2 * t + h
+
+    pass_out(0)
+    for k, h in ((3, 0), (1, 1)):
+        ref, number = values_of(k, h)
+        send(ref, ref, VALUE, number, s, yx, (z + 4 - k) % 4)
+    send_out(1)
     wait(route.at[pl.ds(0, 7)], ROUTE, 0)
     a, b = iota((512, 512), 0), iota((512, 512), 1)
     deal = jnp.where(b == ((a % 16) // 2) * 64 + (a // 16) * 2 + a % 2, 1.0, 0.0).astype(BF)
@@ -210,64 +246,101 @@
             t = (at + k) % 4
             to = y * 4 + t if along == 0 else t * 4 + x
             send(column(t), tables.at[along, at], TABLE, along, s, to, z)
-    wait(wo.at[half], OUT_OVER, 0)
-
-    def of(ref, t, along):
-        return ref.at[:, t, :, 0:896] if along == 0 else ref.at[t, :, :, 896:1792]
+    wait(wo.at[half, 0:1280], OUT_OVER, 0)
+
+    place_on = (x, y)
+    buffers = ((orecv, tsend, trecv), (orecv_on, tsend_on, trecv_on))
+
+    def of(ref, t, along, c):
+        start, width = parts[c]
+        cols = slice(start + along * width // 2, start + (along + 1) * width // 2)
+        return ref.at[:, t, :, cols] if along == 0 else ref.at[t, :, :, cols]
 
     def chip(t, along):
         return y * 4 + t if along == 0 else t * 4 + x
 
-    place_on = (x, y)
-    for pp in range(2):
-        p = (z // 2 + pp) % 2
-        for e in range(2):
-            @pl.when(2 * p + e != z)
-            def _():
-                wait(vals.at[2 * p + e], VALUE, 2 * p + e)
-
-        def project(c, carry):
-            at = pl.ds(pl.multiple_of(c * 256, 256), 256)
+    def project(c, p):
+        def block(b, carry):
+            at = pl.ds(pl.multiple_of(b * 256, 256), 256)
             got = dot(vals[pl.ds(2 * p, 2)].reshape(256, 1024), wo[:, at]).reshape(2, 16, 8, 256)
             osend[p, :, :, :, at] = jnp.concatenate([got[0], got[1]], axis=1).astype(BF).reshape(4, 4, 16, 256)
             return carry
 
-        lax.fori_loop(0, 7, project, 0)
+        lax.fori_loop(parts[c][0] // 256, sum(parts[c]) // 256, block, 0)
         for along in range(2):
             at = place_on[along]
-            keep(of(osend.at[p], at, along), orecv.at[p, along, at], SUM, 2 * p + along)
+            number = 4 * c + 2 * p + along
+            there = buffers[c][0].at[p, along, at]
+            keep(of(osend.at[p], at, along, c), there, SUM, number)
             for k in (1, 3, 2):
                 t = (at + k) % 4
-                send(of(osend.at[p], t, along), orecv.at[p, along, at], SUM, 2 * p + along, s, chip(t, along), z)
-
-    for pp in range(2):
-        p = (z // 2 + pp) % 2
+                send(of(osend.at[p], t, along, c), there, SUM, number, s, chip(t, along), z)
+
+    def sum_on(c, p):
+        first, middle, last = buffers[c]
         for along in range(2):
-            wait(orecv.at[p, along], SUM, 2 * p + along)
-            got = [orecv[p, along, i].astype(F32) for i in range(4)]
-            tsend[p, along] = ((got[0] + got[1]) + (got[2] + got[3])).astype(BF)
+            number = 4 * c + 2 * p + along
+            wait(first.at[p, along], SUM, number)
+            got = [first[p, along, i].astype(F32) for i in range(4)]
+            middle[p, along] = ((got[0] + got[1]) + (got[2] + got[3])).astype(BF)
             at = place_on[1 - along]
-            keep(tsend.at[p, along, at], trecv.at[p, along, at], SUM_ON, 2 * p + along)
+            there = last.at[p, along, at]
+            keep(middle.at[p, along, at], there, SUM_ON, number)
             for k in (1, 3, 2):
                 t = (at + k) % 4
-                send(
-                    tsend.at[p, along, t], trecv.at[p, along, at],
-                    SUM_ON, 2 * p + along, s, chip(t, 1 - along), z,
-                )
+                send(middle.at[p, along, t], there, SUM_ON, number, s, chip(t, 1 - along), z)
+
+    def row_cols(t, c):
+        start, width = parts[c]
+        return pl.ds(pl.multiple_of(t * 1792 + start, 256), width)
+
+    def finish_sum(c):
+        start, width = parts[c]
+        last = buffers[c][2]
+        for pp in range(2):
+            p = (z // 2 + pp) % 2
+            line = pl.ds(pl.multiple_of(p * 16, 16), 16)
+            for along in range(2):
+                wait(last.at[p, along], SUM_ON, 4 * c + 2 * p + along)
+                got = [last[p, along, i].astype(F32) for i in range(4)]
+                cols = slice(start + along * width // 2, start + (along + 1) * width // 2)
+                base = jnp.concatenate([rrecv[2 * p, :, cols], rrecv[2 * p + 1, :, cols]], axis=0)
+                total = base + ((got[0] + got[1]) + (got[2] + got[3]))
+                at = pl.ds(pl.multiple_of(z * 1792 + start + along * width // 2, 128), width // 2)
+                gathered[s, line, at] = total.astype(BF)
+        mine = gathered.at[s, :, row_cols(z, c)]
+        for k in (1, 3, 2):
+            send(mine, mine, SLICE, c, s, yx, (z + k) % 4)
+        for k in (0, 1, 3, 2) if c == 1 else (0,):
+            send(mine, mine, ROWS_OVER, c, 1 - s, yx, (z + k) % 4)
+
+    def pass_rows(c):
+        width = parts[c][1]
+        wait(gathered.at[s, :, pl.ds(0, 3 * width)], SLICE, c)
+        for k in (1, 3, 2) if c == 0 else ():
+            ref = gathered.at[s, :, row_cols((z + k) % 4, c)]
+            send(ref, ref, ROWS_OVER, c, 1 - s, yx, z)
 
     wait(rrecv, RESID, 0)
-    for pp in range(2):
-        p = (z // 2 + pp) % 2
-        line = pl.ds(pl.multiple_of(p * 16, 16), 16)
-        for along in range(2):
-            wait(trecv.at[p, along], SUM_ON, 2 * p + along)
-            got = [trecv[p, along, i].astype(F32) for i in range(4)]
-            cols = slice(along * 896, along * 896 + 896)
-            base = jnp.concatenate([rrecv[2 * p, :, cols], rrecv[2 * p + 1, :, cols]], axis=0)
-            total = base + ((got[0] + got[1]) + (got[2] + got[3]))
-            gathered[s, line, pl.ds(pl.multiple_of(z * 1792 + along * 896, 128), 896)] = total.astype(BF)
-        for k in (1, 3, 2):
-            send(gathered.at[s, line, here], gathered.at[s, line, here], SLICE, p, s, yx, (z + k) % 4)
+    own_p = z // 2
+    values_of(1, 0)
+    values_of(3, 1)
+    project(0, own_p)
+    values_of(2, 0)
+    values_of(2, 1)
+    project(0, 1 - own_p)
+    sum_on(0, own_p)
+    sum_on(0, 1 - own_p)
+    pass_out(1)
+    wait(wo.at[half, 1280:1792], OUT_OVER, 1)
+    project(1, own_p)
+    project(1, 1 - own_p)
+    finish_sum(0)
+    sum_on(1, own_p)
+    sum_on(1, 1 - own_p)
+    pass_rows(0)
+    finish_sum(1)
+    pass_rows(1)
 
     def norm(core, p):
         stream = gathered[core, pl.ds(pl.multiple_of(p * 16, 16), 16)].astype(F32)
@@ -275,16 +348,12 @@
         at = pl.ds(pl.multiple_of(core * 32 + p * 16, 16), 16)
         normed[at] = (stream * lax.rsqrt(mean + 1e-06) * gain[...]).astype(BF)
 
-    for pp in range(2):
-        p = (z // 2 + pp) % 2
-        line = pl.ds(pl.multiple_of(p * 16, 16), 16)
-        wait(gathered.at[s, line, pl.ds(0, 5376)], SLICE, p)
-        send(gathered.at[s, line], gathered.at[s, line], ROWS_OVER, p, 1 - s, yx, z)
-        norm(s, p)
-    for pp in range(2):
-        p = (z // 2 + pp) % 2
-        wait(gathered.at[s, pl.ds(0, 16)], ROWS_OVER, p)
-        norm(1 - s, p)
+    norm(s, 0)
+    norm(s, 1)
+    wait(gathered.at[s, :, pl.ds(0, 5120)], ROWS_OVER, 0)
+    wait(gathered.at[s, :, pl.ds(0, 2048)], ROWS_OVER, 1)
+    norm(1 - s, 0)
+    norm(1 - s, 1)
 
     land = pl.ds(pl.multiple_of(yx * 16, 16), 16)
     flat = select[...].reshape(512, 128)[:, 0:64]
@@ -507,7 +576,9 @@
         (late.at[:, pl.ds(0, 15)], LATENT),
         (vals.at[pl.ds(0, 3)], VALUE),
         (orecv.at[:, :, pl.ds(0, 3)], SUM),
+        (orecv_on.at[:, :, pl.ds(0, 3)], SUM),
         (tsend.at[:, :, pl.ds(0, 3)], SUM_ON),
+        (tsend_on.at[:, :, pl.ds(0, 3)], SUM_ON),
         (gathered.at[s, :, pl.ds(0, 5376)], SLICE),
         (gathered.at[s], ROWS_OVER),
         (route.at[pl.ds(0, 7)], ROUTE),
@@ -538,15 +609,19 @@
 ):
     scratch = [
         pltpu.VMEM((8, 576, 512), BF),
+        pltpu.VMEM((8, 576, 128), BF),
         pltpu.VMEM((4, 16, 16, 512), BF),
         pltpu.VMEM((16, 4, 16, 512), BF),
         pltpu.VMEM((512, 1024), BF),
         pltpu.VMEM((1024, 1792), BF),
         pltpu.VMEM((4, 4, 32, 1024), BF),
         pltpu.VMEM((2, 4, 4, 16, 1792), BF),
-        pltpu.VMEM((2, 2, 4, 4, 16, 896), BF),
-        pltpu.VMEM((2, 2, 4, 16, 896), BF),
-        pltpu.VMEM((2, 2, 4, 16, 896), BF),
+        pltpu.VMEM((2, 2, 4, 4, 16, 640), BF),
+        pltpu.VMEM((2, 2, 4, 4, 16, 256), BF),
+        pltpu.VMEM((2, 2, 4, 16, 640), BF),
+        pltpu.VMEM((2, 2, 4, 16, 256), BF),
+        pltpu.VMEM((2, 2, 4, 16, 640), BF),
+        pltpu.VMEM((2, 2, 4, 16, 256), BF),
         pltpu.VMEM((4, 8, 1792), F32),
         pltpu.VMEM((4, 8, 1792), F32),
         pltpu.VMEM((2, 32, 7168), BF),
@@ -574,11 +649,11 @@
         pltpu.VMEM((32, 16, 384), BF),
         pltpu.VMEM((8, 16, 1280), BF),
         pltpu.VMEM((8, 16, 1280), BF),
-    ] + [pltpu.SemaphoreType.DMA((n,)) for n in (11, len(PARTS), sum(PARTS))]
+    ] + [pltpu.SemaphoreType.DMA((n,)) for n in (19, len(PARTS), sum(PARTS))]
     both = pl.pallas_call(
         kernel,
         out_shape=jax.ShapeDtypeStruct((2, 8, 7168), BF),
-        in_specs=[SMEM] * 4 + [VMEM, ANY, ANY, ANY, VMEM, VMEM, ANY, ANY, ANY],
+        in_specs=[SMEM, SMEM, VMEM, SMEM, ANY, ANY, ANY, ANY, VMEM, VMEM, ANY, ANY, ANY],
         out_specs=VMEM,
         scratch_shapes=scratch,
         compiler_params=pltpu.CompilerParams(collective_id=0, has_side_effects=True, vmem_limit_bytes=60 * MB),
@@ -586,7 +661,7 @@
     )(
         lengths,
         expert_ids.T,
-        gate_weights.T.astype(F32),
+        gate_weights.T,
         replica_slot.T,
         jnp.swapaxes(queries, 1, 2),
         jnp.swapaxes(cache, 1, 2),

time: 140 us -> 134 us (0.957)
  Pallas kernels: 136 us -> 132 us
    pallas_call x1, Pallas kernels: 136 us -> 132 us  [local(): pl.pallas_call(kernel, out_shape=jax.ShapeDtypeStruct((2, 8, 7168), BF),...]
where the time goes in v4:
time: 134 us
  Pallas kernels  132 us (99%)
  local copies, waits for them, and re-layouts  1.65 us (1%)
    pallas_call x1, Pallas kernels, local(): pl.pallas_call(kernel, out_shape=jax.ShapeDtypeStruct((2, 8, 7168), BF),...  132 us

profile of v4, /device:TPU:1, one launch (start us, length us, event | category | flops | bytes accessed | tf_op | source)
XLA Modules:
  0.0 133.9 jit_solution(4334070123153110881)
XLA Ops:
  0.6 131.6 %layer.1 = bf16[2,8,7168]{2,1,0:T(8,128)(2,1)} custom-call(s32[8]{0:T(128)} %lengths.1, s32[4,8]{1,0:T(4,128)} %bitcast.21, bf16[4,8]{1,0:T(4,128)(2,1)} %bitcast.22, s32[2,24]{1,0:T(2,128)} %bitcast.23, bf16[8,576,128]{2,1,0:T(8,128)(2,1)} %bitcast.18, bf16[8,576,512]{2,1,0:T(8,128)(2,1)} %bitcast.14, bf16[512,128]{1,0:T(8,128)(2,1)} %bitcast.19, ...), custom_call_target="tpu_custom_call" | custom-call | tf_op jit(solution)/shard_map/layer/pallas_call | solution.py:653
  132.2 1.7 %slice_bitcast_fusion = (bf16[8,7168]{1,0:T(8,128)(2,1)}, bf16[8,7168]{1,0:T(8,128)(2,1)}) fusion(bf16[2,8,7168]{2,1,0:T(8,128)(2,1)} %layer.1), kind=kLoop, calls=%fused_computation | loop fusion | bytes 458752 | tf_op jit(solution)/shard_map/squeeze | solution.py:676

commit v5 on v4

--- a/solution.py
+++ b/solution.py
@@ -33,7 +33,7 @@
 
 
 W_UV, W_OUT, RESID, UV_OVER, OUT_OVER, LATENT, VALUE, SUM, SLICE, ROWS_OVER, ROUTE, PICK, PICK_REST, GATHER, PIECE, BACK, RESULT, SUM_ON, TABLE, LINES, HOME, HOME_ON = range(22)
-PARTS = (8, 8, 1, 1, 2, 1, 8, 8, 2, 2, 1, 2, 4, 8, 4, 1, 1, 8, 2, 4, 4, 4)
+PARTS = (8, 8, 1, 1, 2, 1, 8, 8, 2, 2, 1, 2, 4, 8, 4, 1, 3, 8, 2, 4, 4, 4)
 FIRST = tuple(sum(PARTS[:i]) for i in range(len(PARTS)))
 
 
@@ -522,30 +522,39 @@
     home(1)
     slices(3)
 
-    for c in range(2):
+    result_cols = (slice(0, 512), slice(512, 1024), slice(1024, 1280))
+
+    def finish(n):
+        cols = result_cols[n]
+        keep(fsend.at[line_me, :, cols], frecv.at[line_me, :, cols], RESULT, n)
+
+        def out(k, carry):
+            core, to = (s + k // 4) % 2, (z + k % 4) % 4
+            send(fsend.at[core * 4 + to, :, cols], frecv.at[line_me, :, cols], RESULT, n, core, yx, to)
+            return carry
+
+        lax.fori_loop(1, 8, out, 0)
+
+    def finish_rest(c):
+        total = []
         for along in range(2):
             wait(trecv_home.at[along, c], HOME_ON, 2 * along + c)
             got = [trecv_home[along, c, i].astype(F32) for i in range(4)]
-            total = (got[0] + got[1]) + (got[2] + got[3])
-            if along == 0:
-                first = total
-            else:
-                both_rows = jnp.concatenate([first.reshape(8, 8, 512), total.reshape(8, 8, 512)], axis=1)
-                fsend[:, :, c * 512 : c * 512 + 512] = both_rows.astype(BF)
-    wait(back, BACK, 0)
-    total = dot(select[...].reshape(512, 128), back[...].reshape(512, 384), ((0,), (0,)))[64:128]
-    low = total[:, 0:256].reshape(8, 8, 256)
-    high = jnp.concatenate([total[:, 256:384], jnp.zeros((64, 128), F32)], axis=1).reshape(8, 8, 256)
-    fsend[:, :, 1024:1280] = jnp.concatenate([low, high], axis=1).astype(BF)
-    keep(fsend.at[line_me], frecv.at[line_me], RESULT, 0)
-
-    def finish(k, carry):
-        core, to = (s + k // 4) % 2, (z + k % 4) % 4
-        send(fsend.at[core * 4 + to], frecv.at[line_me], RESULT, 0, core, yx, to)
-        return carry
-
-    lax.fori_loop(1, 8, finish, 0)
-    wait(frecv, RESULT, 0)
+            total.append(((got[0] + got[1]) + (got[2] + got[3])).reshape(8, 8, 512))
+        fsend[:, :, result_cols[c]] = jnp.concatenate(total, axis=1).astype(BF)
+        finish(c)
+
+    def finish_slices():
+        wait(back, BACK, 0)
+        total = dot(select[...].reshape(512, 128), back[...].reshape(512, 384), ((0,), (0,)))[64:128]
+        low = total[:, 0:256].reshape(8, 8, 256)
+        high = jnp.concatenate([total[:, 256:384], jnp.zeros((64, 128), F32)], axis=1).reshape(8, 8, 256)
+        fsend[:, :, 1024:1280] = jnp.concatenate([low, high], axis=1).astype(BF)
+        finish(2)
+
+    finish_rest(0)
+    finish_rest(1)
+    finish_slices()
 
     def write(first, width, moe):
         at = slice(first, first + width)
@@ -556,16 +565,18 @@
         both[0, :, at] = own.astype(BF)
         both[1, :, at] = (own + moe).astype(BF)
 
+    for c in range(2):
+        wait(frecv.at[:, :, result_cols[c]], RESULT, c)
+        for core in range(2):
+            got = [frecv[core * 4 + t, :, result_cols[c]].astype(F32) for t in range(4)]
+            total = (got[0] + got[1]) + (got[2] + got[3])
+            write(3072 + core * 2048 + c * 512, 512, total[0:8])
+            write(3072 + core * 2048 + 1024 + c * 512, 512, total[8:16])
+    wait(frecv.at[:, :, result_cols[2]], RESULT, 2)
     for j in range(8):
         got = frecv[(j % 2) * 4 + j // 2, :, 1024:1280].astype(F32)
         write(j * 384, 256, got[0:8])
         write(j * 384 + 256, 128, got[8:16, 0:128])
-    for core in range(2):
-        for c in range(2):
-            got = [frecv[core * 4 + t, :, c * 512 : c * 512 + 512].astype(F32) for t in range(4)]
-            total = (got[0] + got[1]) + (got[2] + got[3])
-            write(3072 + core * 2048 + c * 512, 512, total[0:8])
-            write(3072 + core * 2048 + 1024 + c * 512, 512, total[8:16])
 
     for ref, kind in (
         (wuv.at[:, pl.ds(0, 384)], W_UV),

time: 134 us -> 132 us (0.985)
  Pallas kernels: 132 us -> 130 us
    pallas_call x1, Pallas kernels: 132 us -> 130 us  [local(): pl.pallas_call(kernel, out_shape=jax.ShapeDtypeStruct((2, 8, 7168), BF),...]
where the time goes in v5:
time: 132 us
  Pallas kernels  130 us (98%)
  local copies, waits for them, and re-layouts  1.65 us (1%)
    pallas_call x1, Pallas kernels, local(): pl.pallas_call(kernel, out_shape=jax.ShapeDtypeStruct((2, 8, 7168), BF),...  130 us

profile of v5, /device:TPU:1, one launch (start us, length us, event | category | flops | bytes accessed | tf_op | source)
XLA Modules:
  0.0 132.0 jit_solution(6015704617063333227)
XLA Ops:
  0.6 129.7 %layer.1 = bf16[2,8,7168]{2,1,0:T(8,128)(2,1)} custom-call(s32[8]{0:T(128)} %lengths.1, s32[4,8]{1,0:T(4,128)} %bitcast.21, bf16[4,8]{1,0:T(4,128)(2,1)} %bitcast.22, s32[2,24]{1,0:T(2,128)} %bitcast.23, bf16[8,576,128]{2,1,0:T(8,128)(2,1)} %bitcast.18, bf16[8,576,512]{2,1,0:T(8,128)(2,1)} %bitcast.14, bf16[512,128]{1,0:T(8,128)(2,1)} %bitcast.19, ...), custom_call_target="tpu_custom_call" | custom-call | tf_op jit(solution)/shard_map/layer/pallas_call | solution.py:664
  130.4 1.7 %slice_bitcast_fusion = (bf16[8,7168]{1,0:T(8,128)(2,1)}, bf16[8,7168]{1,0:T(8,128)(2,1)}) fusion(bf16[2,8,7168]{2,1,0:T(8,128)(2,1)} %layer.1), kind=kLoop, calls=%fused_computation | loop fusion | bytes 458752 | tf_op jit(solution)/shard_map/squeeze | solution.py:687

commit v6 on v5

--- a/solution.py
+++ b/solution.py
@@ -33,7 +33,7 @@
 
 
 W_UV, W_OUT, RESID, UV_OVER, OUT_OVER, LATENT, VALUE, SUM, SLICE, ROWS_OVER, ROUTE, PICK, PICK_REST, GATHER, PIECE, BACK, RESULT, SUM_ON, TABLE, LINES, HOME, HOME_ON = range(22)
-PARTS = (8, 8, 1, 1, 2, 1, 8, 8, 2, 2, 1, 2, 4, 8, 4, 1, 3, 8, 2, 4, 4, 4)
+PARTS = (8, 8, 1, 1, 2, 1, 8, 8, 2, 2, 1, 2, 4, 16, 4, 1, 3, 8, 2, 4, 4, 4)
 FIRST = tuple(sum(PARTS[:i]) for i in range(len(PARTS)))
 
 
@@ -407,11 +407,21 @@
                     send(rest.at[along, c, core, t], place_in, PICK_REST, 2 * along + c, core, chip(t, 1 - along), z)
             send(rest.at[along, c, 1 - s, at], place_in, PICK_REST, 2 * along + c, 1 - s, yx, z)
 
+    def spread_part(t, c, h):
+        return rows.at[2 * h : 2 * h + 2, :, :, whole_cols(t, c)], 8 * c + 2 * t + h
+
     def spread(c):
-        cols = whole_cols(z, c)
-        wait(rows.at[:, :, :, cols], PICK, c)
-        for k in (1, 3, 2):
-            send(rows.at[:, :, :, cols], rows.at[:, :, :, cols], GATHER, c * 4 + z, s, yx, (z + k) % 4)
+        wait(rows.at[:, :, :, whole_cols(z, c)], PICK, c)
+        for h in range(2):
+            ref, number = spread_part(z, c, h)
+            for k in (1, 3):
+                send(ref, ref, GATHER, number, s, yx, (z + k) % 4)
+
+    def spread_on(c):
+        for k, h in ((3, 0), (1, 1)):
+            ref, number = spread_part((z + k) % 4, c, h)
+            wait(ref, GATHER, number)
+            send(ref, ref, GATHER, number, s, yx, (z + 4 - k) % 4)
 
     wait(tables.at[0], TABLE, 0)
     wait(tables.at[1], TABLE, 1)
@@ -422,7 +432,9 @@
     spread(0)
     deliver_rest(0)
     spread(1)
+    spread_on(0)
     deliver_rest(1)
+    spread_on(1)
 
     pltpu.make_async_copy(w_gate, wg, csem.at[8]).wait()
     pltpu.make_async_copy(w_up, wu, csem.at[9]).wait()
@@ -438,7 +450,10 @@
     for c in range(2):
         for k in (1, 3, 2):
             t = (z + k) % 4
-            wait(rows.at[:, :, :, whole_cols(t, c)], GATHER, c * 4 + t)
+            for h in range(2):
+                if (k, h) not in ((3, 0), (1, 1)):
+                    ref, number = spread_part(t, c, h)
+                    wait(ref, GATHER, number)
             enter(whole_cols(t, c))
         for along in range(2):
             wait(rows.at[:, :, :, pl.ds(0, 1024)], PICK_REST, 2 * along + c)

time: 132 us -> 131 us (level)
  no operation moved by 1% of the time
where the time goes in v6:
time: 131 us
  Pallas kernels  129 us (98%)
  local copies, waits for them, and re-layouts  1.65 us (1%)
    pallas_call x1, Pallas kernels, local(): pl.pallas_call(kernel, out_shape=jax.ShapeDtypeStruct((2, 8, 7168), BF),...  129 us

profile of v6, /device:TPU:1, one launch (start us, length us, event | category | flops | bytes accessed | tf_op | source)
XLA Modules:
  0.0 131.3 jit_solution(5164500164800608741)
XLA Ops:
  0.6 129.0 %layer.1 = bf16[2,8,7168]{2,1,0:T(8,128)(2,1)} custom-call(s32[8]{0:T(128)} %lengths.1, s32[4,8]{1,0:T(4,128)} %bitcast.21, bf16[4,8]{1,0:T(4,128)(2,1)} %bitcast.22, s32[2,24]{1,0:T(2,128)} %bitcast.23, bf16[8,576,128]{2,1,0:T(8,128)(2,1)} %bitcast.18, bf16[8,576,512]{2,1,0:T(8,128)(2,1)} %bitcast.14, bf16[512,128]{1,0:T(8,128)(2,1)} %bitcast.19, ...), custom_call_target="tpu_custom_call" | custom-call | tf_op jit(solution)/shard_map/layer/pallas_call | solution.py:679
  129.6 1.7 %slice_bitcast_fusion = (bf16[8,7168]{1,0:T(8,128)(2,1)}, bf16[8,7168]{1,0:T(8,128)(2,1)}) fusion(bf16[2,8,7168]{2,1,0:T(8,128)(2,1)} %layer.1), kind=kLoop, calls=%fused_computation | loop fusion | bytes 458752 | tf_op jit(solution)/shard_map/squeeze | solution.py:702

commit v7 on v6

--- a/solution.py
+++ b/solution.py
@@ -568,8 +568,8 @@
         finish(2)
 
     finish_rest(0)
+    finish_slices()
     finish_rest(1)
-    finish_slices()
 
     def write(first, width, moe):
         at = slice(first, first + width)

time: 131 us -> 132 us (level)
  no operation moved by 1% of the time
where the time goes in v7:
time: 132 us
  Pallas kernels  129 us (98%)
  local copies, waits for them, and re-layouts  1.65 us (1%)
    pallas_call x1, Pallas kernels, local(): pl.pallas_call(kernel, out_shape=jax.ShapeDtypeStruct((2, 8, 7168), BF),...  129 us

profile of v7, /device:TPU:1, one launch (start us, length us, event | category | flops | bytes accessed | tf_op | source)
XLA Modules:
  0.0 131.6 jit_solution(10028083717949681434)
XLA Ops:
  0.6 129.3 %layer.1 = bf16[2,8,7168]{2,1,0:T(8,128)(2,1)} custom-call(s32[8]{0:T(128)} %lengths.1, s32[4,8]{1,0:T(4,128)} %bitcast.21, bf16[4,8]{1,0:T(4,128)(2,1)} %bitcast.22, s32[2,24]{1,0:T(2,128)} %bitcast.23, bf16[8,576,128]{2,1,0:T(8,128)(2,1)} %bitcast.18, bf16[8,576,512]{2,1,0:T(8,128)(2,1)} %bitcast.14, bf16[512,128]{1,0:T(8,128)(2,1)} %bitcast.19, ...), custom_call_target="tpu_custom_call" | custom-call | tf_op jit(solution)/shard_map/layer/pallas_call | solution.py:679
  130.0 1.7 %slice_bitcast_fusion = (bf16[8,7168]{1,0:T(8,128)(2,1)}, bf16[8,7168]{1,0:T(8,128)(2,1)}) fusion(bf16[2,8,7168]{2,1,0:T(8,128)(2,1)} %layer.1), kind=kLoop, calls=%fused_computation | loop fusion | bytes 458752 | tf_op jit(solution)/shard_map/squeeze | solution.py:702
